TPU v7x, 32 devices: a whole 2x2x4 slice. The times are simulated.
32 devices in a mesh: section: 2 (over y), dp: 4 (over z), tensor: 4 (over x, core).
Axes of the slice: x: 2, y: 2, z: 4, core: 2. Of those that a mesh axis runs over, the one named last changes fastest.
Arguments:
- frames: bfloat16 [2, 1024, 1024], P(None, 'dp', 'tensor'), may hold values from -6 to 6
- cotangent: bfloat16 [2, 1024, 1024], P(None, 'dp', 'tensor'), may hold values from -6 to 6
- lengths: int32 [2, 4, 2], P(None, 'dp'), may hold values from 0 to 256, as said below
- norm1_gain: float32 [2, 1024], P('section'), may hold values from 0.5 to 1.5
- norm1_bias: float32 [2, 1024], P('section'), may hold values from -1.5 to 1.5
- norm2_gain: float32 [2, 1024], P('section'), may hold values from 0.5 to 1.5
- norm2_bias: float32 [2, 1024], P('section'), may hold values from -1.5 to 1.5
- w_qkv: bfloat16 [2, 1024, 3072], P('section', None, 'tensor'), may hold values from -0.1875 to 0.1875
- w_out: bfloat16 [2, 1024, 1024], P('section', 'tensor'), may hold values from -0.75 to 0.75
- w_up: bfloat16 [2, 1024, 4096], P('section', None, 'tensor'), may hold values from -0.1875 to 0.1875
- w_down: bfloat16 [2, 4096, 1024], P('section', 'tensor'), may hold values from -0.09375 to 0.09375
- w_skip: bfloat16 [2, 1024, 1024], P('section', None, 'tensor'), may hold values from -0.125 to 0.125
Outputs:
- boundary: bfloat16 [2, 2, 1024, 1024], P('section', None, 'dp', 'tensor')
- grad_norm1_gain: float32 [2, 1024], P('section')
- grad_norm1_bias: float32 [2, 1024], P('section')
- grad_norm2_gain: float32 [2, 1024], P('section')
- grad_norm2_bias: float32 [2, 1024], P('section')
- grad_qkv_weight: float32 [2, 1024, 3072], P('section', None, 'tensor')
- grad_out_weight: float32 [2, 1024, 1024], P('section', 'tensor')
- grad_up_weight: float32 [2, 1024, 4096], P('section', None, 'tensor')
- grad_down_weight: float32 [2, 4096, 1024], P('section', 'tensor')
- grad_skip_weight: float32 [2, 1024, 1024], P('section', None, 'tensor')
Inputs may be any that keep to these rules, and one draw needn't show every extreme that they name: In each block the two lengths add up to at most 256; the first is at least 64; the second may be 0. In every micro-batch one index of dp has a first utterance of exactly 256 frames.
All inputs are finite; a program needn't handle non-finite values.
Results may differ from a plain program's by a relative error of at most 0.038.
Values may be sent and summed in bfloat16 or wider, within the bound.
No kernel may reach another device: no remote copies, remote signals or barrier semaphores. Data moves between devices by JAX's collectives and lax.ppermute only.
A program may use at most 128 MiB of HBM per device.

v0:
```python
import jax
import jax.numpy as jnp
from jax import lax
from jax.sharding import PartitionSpec as P

HEADS = 16
HD = 64
UTT = 2


epsilon = 1e-05
inv_root_two = 0.7071067811865476
inv_root_two_pi = 0.3989422804014327


def from_behind(value, axis, steps):
    count = lax.axis_size(axis)
    first, last = (max(0, -steps), min(count, count - steps))
    return lax.ppermute(value, axis, [(source, source + steps) for source in range(first, last)])


def product(left, right):
    return jnp.dot(left, right, preferred_element_type=jnp.float32)


def product_tn(left, right):
    return lax.dot_general(
        left, right, (((0,), (0,)), ((), ())), preferred_element_type=jnp.float32
    )


def product_nt(left, right):
    return lax.dot_general(
        left, right, (((1,), (1,)), ((), ())), preferred_element_type=jnp.float32
    )


def reduce_rows(partial_sum):
    return lax.psum_scatter(
        partial_sum.astype(jnp.bfloat16), "tensor", scatter_dimension=0, tiled=True
    ).astype(jnp.float32)


def whole_rows(rounded):
    return lax.all_gather(rounded, "tensor", axis=0, tiled=True)


def row_share(full_rows):
    share = full_rows.shape[0] // lax.axis_size("tensor")
    return lax.dynamic_slice_in_dim(full_rows, lax.axis_index("tensor") * share, share, 0)


def to_rows(column_block):
    return lax.all_to_all(
        column_block.astype(jnp.bfloat16), "tensor", split_axis=0, concat_axis=1, tiled=True
    ).astype(column_block.dtype)


def to_columns(rounded):
    return lax.all_to_all(rounded, "tensor", split_axis=1, concat_axis=0, tiled=True)


def norm_stats(inputs):
    average = jnp.mean(inputs, -1, keepdims=True)
    centred = inputs - average
    inverse = lax.rsqrt(jnp.mean(centred * centred, -1, keepdims=True) + epsilon)
    return (centred * inverse, inverse)


def norm_back(grad_norm, normed, inverse, gain):
    scaled = grad_norm * gain
    return inverse * (
        scaled
        - jnp.mean(scaled, -1, keepdims=True)
        - normed * jnp.mean(scaled * normed, -1, keepdims=True)
    )


def score_block(queries, keys_all, slopes, allowed):
    raw_scores = jnp.einsum("qhd,khd->hqk", queries, keys_all, preferred_element_type=jnp.float32)
    positions = jnp.arange(queries.shape[0], dtype=jnp.int32)
    distance = jnp.abs(positions[:, None] - positions[None, :]).astype(jnp.float32)
    scores = raw_scores * HD ** (-0.5) - slopes[:, None, None] * distance[None]
    return jnp.where(allowed[None], scores, -1e30)


def layer_forward(inputs, weights, allowed, slopes):
    gain_one, bias_one, gain_two, bias_two, w_qkv, w_out, w_up, w_down = weights
    heads_here = w_qkv.shape[1] // (3 * HD)
    normed_one, inv_one = norm_stats(inputs)
    attn_in = whole_rows((normed_one * gain_one + bias_one).astype(jnp.bfloat16))
    rows_count = attn_in.shape[0]
    packed = product(attn_in, w_qkv).astype(jnp.bfloat16).reshape(rows_count, heads_here, 3, HD)
    scores = score_block(packed[:, :, 0], packed[:, :, 1], slopes, allowed)
    top_score = jnp.max(scores, -1, keepdims=True)
    exp_scores = jnp.exp(scores - top_score)
    exp_total = jnp.sum(exp_scores, -1, keepdims=True)
    log_total = top_score + jnp.log(exp_total)
    attn_probs = exp_scores / exp_total
    head_mix = jnp.einsum(
        "hqk,khd->qhd",
        attn_probs.astype(jnp.bfloat16),
        packed[:, :, 2],
        preferred_element_type=jnp.float32,
    )
    head_mix = head_mix.astype(jnp.bfloat16).reshape(rows_count, heads_here * HD)
    middle = inputs + reduce_rows(product(head_mix, w_out))
    normed_two, inv_two = norm_stats(middle)
    ffn_in = whole_rows((normed_two * gain_two + bias_two).astype(jnp.bfloat16))
    pre_act = product(ffn_in, w_up)
    activated = jax.nn.gelu(pre_act, approximate=False).astype(jnp.bfloat16)
    branch = reduce_rows(product(activated, w_down))
    kept_acts = (
        normed_one,
        inv_one,
        attn_in,
        packed,
        log_total,
        head_mix,
        normed_two,
        inv_two,
        ffn_in,
        pre_act,
        activated,
    )
    return (middle + branch, kept_acts)


def layer_backward(grad_out, kept_acts, weights, allowed, slopes):
    gain_one, bias_one, gain_two, bias_two, w_qkv, w_out, w_up, w_down = weights
    (
        normed_one,
        inv_one,
        attn_in,
        packed,
        log_total,
        head_mix,
        normed_two,
        inv_two,
        ffn_in,
        pre_act,
        activated,
    ) = kept_acts
    heads_here = w_qkv.shape[1] // (3 * HD)
    grad_branch = whole_rows(grad_out.astype(jnp.bfloat16))
    rows_count = grad_branch.shape[0]
    grad_down = product_tn(activated, grad_branch)
    grad_act = product_nt(grad_branch, w_down)
    normal_cdf = 0.5 * (1.0 + lax.erf(pre_act * inv_root_two))
    normal_pdf = jnp.exp(-0.5 * pre_act * pre_act) * inv_root_two_pi
    grad_pre = (grad_act * (normal_cdf + pre_act * normal_pdf)).astype(jnp.bfloat16)
    grad_up = product_tn(ffn_in, grad_pre)
    grad_norm_two = reduce_rows(product_nt(grad_pre, w_up))
    grad_gain_two = jnp.sum(grad_norm_two * normed_two, 0)
    grad_bias_two = jnp.sum(grad_norm_two, 0)
    grad_mid = grad_out + norm_back(grad_norm_two, normed_two, inv_two, gain_two)
    grad_attn = whole_rows(grad_mid.astype(jnp.bfloat16))
    grad_outw = product_tn(head_mix, grad_attn)
    grad_mix = product_nt(grad_attn, w_out).astype(jnp.bfloat16).reshape(rows_count, heads_here, HD)
    queries = packed[:, :, 0]
    keys_all = packed[:, :, 1]
    values = packed[:, :, 2]
    attn_probs = jnp.exp(score_block(queries, keys_all, slopes, allowed) - log_total)
    grad_probs = jnp.einsum("qhd,khd->hqk", grad_mix, values, preferred_element_type=jnp.float32)
    row_delta = jnp.sum(attn_probs * grad_probs, -1, keepdims=True)
    grad_scores = (attn_probs * (grad_probs - row_delta)).astype(jnp.bfloat16)
    grad_values = jnp.einsum(
        "hqk,qhd->khd",
        attn_probs.astype(jnp.bfloat16),
        grad_mix,
        preferred_element_type=jnp.float32,
    )
    grad_queries = jnp.einsum(
        "hqk,khd->qhd", grad_scores, keys_all, preferred_element_type=jnp.float32
    ) * HD ** (-0.5)
    grad_keys = jnp.einsum(
        "hqk,qhd->khd", grad_scores, queries, preferred_element_type=jnp.float32
    ) * HD ** (-0.5)
    grad_packed = jnp.stack([grad_queries, grad_keys, grad_values], 2).astype(jnp.bfloat16)
    grad_packed = grad_packed.reshape(rows_count, heads_here * 3 * HD)
    grad_qkvw = product_tn(attn_in, grad_packed)
    grad_norm_one = reduce_rows(product_nt(grad_packed, w_qkv))
    grad_gain_one = jnp.sum(grad_norm_one * normed_one, 0)
    grad_bias_one = jnp.sum(grad_norm_one, 0)
    grad_in = grad_mid + norm_back(grad_norm_one, normed_one, inv_one, gain_one)
    return (
        grad_in,
        (
            grad_gain_one,
            grad_bias_one,
            grad_gain_two,
            grad_bias_two,
            grad_qkvw,
            grad_outw,
            grad_up,
            grad_down,
        ),
    )


def shards(
    frames,
    cotangent,
    lengths,
    norm1_gain,
    norm1_bias,
    norm2_gain,
    norm2_bias,
    w_qkv,
    w_out,
    w_up,
    w_down,
    w_skip,
):
    section_at = lax.axis_index("section")
    first_section = section_at == 0
    column_at = lax.axis_index("tensor")
    whole_in, whole_cot = (
        lax.all_gather(frames, "tensor", axis=2, tiled=True),
        lax.all_gather(cotangent, "tensor", axis=2, tiled=True),
    )
    micro_count = frames.shape[0]
    rows_count = frames.shape[1]
    quarter = frames.shape[2]
    full_width = whole_in.shape[2]
    weights = (
        norm1_gain[0],
        norm1_bias[0],
        norm2_gain[0],
        norm2_bias[0],
        w_qkv[0],
        w_out[0],
        w_up[0],
        w_down[0],
    )
    skip_weight = w_skip[0]
    heads_here = w_qkv.shape[2] // (3 * HD)
    head_ids = column_at * heads_here + jnp.arange(heads_here, dtype=jnp.int32)
    slopes = 2.0 ** (-8.0 * (head_ids + 1).astype(jnp.float32) / HEADS)
    positions = jnp.arange(rows_count, dtype=jnp.int32)

    def segment_of(batch_at):
        utt_ends = jnp.cumsum(lengths[batch_at, 0])
        return jnp.sum((positions[:, None] >= utt_ends[None, :]).astype(jnp.int32), -1)

    recv_rows = row_share(jnp.zeros((rows_count, full_width), jnp.bfloat16))
    recv_part = jnp.zeros((rows_count, quarter), jnp.float32)
    saved_steps = []
    for fwd_step in range(micro_count + 1):
        own_index = min(fwd_step, micro_count - 1)
        other_index = max(fwd_step - 1, 0)
        segment = jnp.where(first_section, segment_of(own_index), segment_of(other_index))
        allowed = segment[:, None] == segment[None, :]
        own_rows = whole_in[own_index]
        proj_in = jnp.where(first_section, own_rows, whole_rows(recv_rows))
        skip_part = product(proj_in, skip_weight)
        joined = to_rows(skip_part + recv_part)
        layer_in = jnp.where(first_section, row_share(own_rows).astype(jnp.float32), joined)
        layer_out, kept_acts = layer_forward(layer_in, weights, allowed, slopes)
        recv_rows = from_behind(layer_out.astype(jnp.bfloat16), "section", 1)
        recv_part = from_behind(skip_part.astype(jnp.bfloat16), "section", 1).astype(
            skip_part.dtype
        )
        saved_steps.append((proj_in, segment, allowed, kept_acts, layer_out))
    totals = [jnp.zeros(item.shape, jnp.float32) for item in weights]
    skip_total = jnp.zeros(skip_weight.shape, jnp.float32)
    recv_grad = row_share(jnp.zeros((rows_count, full_width), jnp.float32))
    recv_cols = jnp.zeros((rows_count, quarter), jnp.bfloat16)
    input_grads = [None] * micro_count
    for back_step in range(micro_count + 1):
        fwd_step = micro_count - back_step
        proj_in, segment, allowed, kept_acts, layer_out = saved_steps[fwd_step]
        later_index = max(fwd_step - 1, 0)
        early_scale = 1.0 if fwd_step <= micro_count - 1 else 0.0
        late_scale = 1.0 if fwd_step >= 1 else 0.0
        valid = row_share((segment < UTT).astype(jnp.float32)[:, None])
        seed_grad = row_share(whole_cot[later_index]).astype(jnp.float32) * valid * late_scale
        grad_out = jnp.where(first_section, recv_grad * early_scale, seed_grad)
        grad_in, layer_grads = layer_backward(grad_out, kept_acts, weights, allowed, slopes)
        totals = [total + grad for total, grad in zip(totals, layer_grads)]
        own_cols = to_columns(grad_in.astype(jnp.bfloat16))
        skip_cols = jnp.where(first_section, recv_cols, own_cols)
        skip_total = skip_total + product_tn(proj_in, skip_cols)
        proj_grad = reduce_rows(product_nt(skip_cols, skip_weight))
        if fwd_step <= micro_count - 1:
            input_grads[fwd_step] = grad_in + proj_grad
        recv_cols = from_behind(own_cols, "section", -1)
        recv_grad = from_behind(proj_grad.astype(jnp.bfloat16), "section", -1).astype(
            proj_grad.dtype
        )
    gain_one, bias_one, gain_two, bias_two, qkv_total, out_total, up_total, down_total = totals
    gain_one, bias_one, gain_two, bias_two = lax.psum(
        (gain_one, bias_one, gain_two, bias_two), "tensor"
    )
    summed = (
        lax.psum(gain_one.astype(jnp.bfloat16), "dp").astype(jnp.float32),
        lax.psum(bias_one.astype(jnp.bfloat16), "dp").astype(jnp.float32),
        lax.psum(gain_two.astype(jnp.bfloat16), "dp").astype(jnp.float32),
        lax.psum(bias_two.astype(jnp.bfloat16), "dp").astype(jnp.float32),
        lax.psum(qkv_total.astype(jnp.bfloat16), "dp").astype(jnp.float32),
        lax.psum(out_total.astype(jnp.bfloat16), "dp").astype(jnp.float32),
        lax.psum(up_total.astype(jnp.bfloat16), "dp").astype(jnp.float32),
        lax.psum(down_total.astype(jnp.bfloat16), "dp").astype(jnp.float32),
        lax.psum(skip_total.astype(jnp.bfloat16), "dp").astype(jnp.float32),
    )
    pieces = []
    for batch_at in range(micro_count):
        chosen = jnp.where(first_section, input_grads[batch_at], saved_steps[batch_at + 1][4])
        pieces.append(to_columns(chosen.astype(jnp.bfloat16)))
    boundary = jnp.stack(pieces, 0)[None]
    return (
        boundary,
        summed[0][None],
        summed[1][None],
        summed[2][None],
        summed[3][None],
        summed[4][None],
        summed[5][None],
        summed[6][None],
        summed[7][None],
        summed[8][None],
    )


def solution(mesh):
    in_specs = (
        P(None, "dp", "tensor"),
        P(None, "dp", "tensor"),
        P(None, "dp", None),
        P("section", None),
        P("section", None),
        P("section", None),
        P("section", None),
        P("section", None, "tensor"),
        P("section", "tensor", None),
        P("section", None, "tensor"),
        P("section", "tensor", None),
        P("section", None, "tensor"),
    )
    out_specs = (
        P("section", None, "dp", "tensor"),
        P("section", None),
        P("section", None),
        P("section", None),
        P("section", None),
        P("section", None, "tensor"),
        P("section", "tensor", None),
        P("section", None, "tensor"),
        P("section", "tensor", None),
        P("section", None, "tensor"),
    )
    return jax.shard_map(shards, mesh=mesh, in_specs=in_specs, out_specs=out_specs, check_vma=False)
```

profile of v0, /device:TPU:0, one launch (start us, length us, event | category | flops | bytes accessed | tf_op | source)
XLA Modules:
  0.0 896.6 jit_solution(11554612026376545971)
XLA Ops:
  10.9 18.3 %all-gather.5.cloned.1.call-done = bf16[2,256,1024]{2,1,0:T(8,128)(2,1)} async-done(((bf16[2,256,256]{2,1,0:T(8,128)(2,1)}), bf16[2,256,1024]{2,1,0:T(8,128)(2,1)}) %all-gather.5.cloned.1.call-update) | async-done | bytes 1048592 | tf_op jit(solution)/shard_map/all_gather | solution.py:219
  31.3 3.5 all-to-all-start
  40.5 6.6 all_gather.51
  54.0 22.4 %reduce-scatter.16.cloned.1.call-done = bf16[64,1024]{1,0:T(8,128)(2,1)} async-done(((bf16[256,1024]{1,0:T(8,128)(2,1)}), bf16[64,1024]{1,0:T(8,128)(2,1)}) %reduce-scatter.16.cloned.1.call-update) | async-done | bytes 131088 | tf_op jit(solution)/shard_map/reduce_scatter | solution.py:39
  77.9 6.9 all_gather.52
  87.3 3.7 fusion.62
  91.2 21.9 %reduce-scatter.18.cloned.1.call-done = bf16[64,1024]{1,0:T(8,128)(2,1)} async-done(((bf16[256,1024]{1,0:T(8,128)(2,1)}), bf16[64,1024]{1,0:T(8,128)(2,1)}) %reduce-scatter.18.cloned.1.call-update) | async-done | bytes 131088 | tf_op jit(solution)/shard_map/reduce_scatter | solution.py:39
  114.1 3.4 collective-permute-start
  121.0 6.5 all_gather.53
  134.0 4.4 all-to-all-done.1
  140.0 6.5 all_gather.54
  154.8 23.4 %reduce-scatter.20.cloned.1.call-done = bf16[64,1024]{1,0:T(8,128)(2,1)} async-done(((bf16[256,1024]{1,0:T(8,128)(2,1)}), bf16[64,1024]{1,0:T(8,128)(2,1)}) %reduce-scatter.20.cloned.1.call-update) | async-done | bytes 131088 | tf_op jit(solution)/shard_map/reduce_scatter | solution.py:39
  179.6 6.8 all_gather.55
  186.4 3.7 fusion.113
  192.5 22.1 %reduce-scatter.22.cloned.1.call-done = bf16[64,1024]{1,0:T(8,128)(2,1)} async-done(((bf16[256,1024]{1,0:T(8,128)(2,1)}), bf16[64,1024]{1,0:T(8,128)(2,1)}) %reduce-scatter.22.cloned.1.call-update) | async-done | bytes 131088 | tf_op jit(solution)/shard_map/reduce_scatter | solution.py:39
  215.6 3.4 collective-permute-start.2
  222.8 8.3 all_gather.56
  238.2 3.9 all-to-all-done.2
  244.2 6.5 all_gather.57
  262.1 7.7 all_gather.58
  269.8 12.8 %reduce-scatter.24.cloned.1.call-done = bf16[64,1024]{1,0:T(8,128)(2,1)} async-done(((bf16[256,1024]{1,0:T(8,128)(2,1)}), bf16[64,1024]{1,0:T(8,128)(2,1)}) %reduce-scatter.24.cloned.1.call-update) | async-done | bytes 131088 | tf_op jit(solution)/shard_map/reduce_scatter | solution.py:39
  284.1 6.8 all_gather.59
  290.9 3.7 fusion.128
  298.1 22.1 %reduce-scatter.26.cloned.1.call-done = bf16[64,1024]{1,0:T(8,128)(2,1)} async-done(((bf16[256,1024]{1,0:T(8,128)(2,1)}), bf16[64,1024]{1,0:T(8,128)(2,1)}) %reduce-scatter.26.cloned.1.call-update) | async-done | bytes 131088 | tf_op jit(solution)/shard_map/reduce_scatter | solution.py:39
  323.9 6.8 all_gather.60
  334.8 22.1 %reduce-scatter.28.cloned.1.call-done = bf16[64,1024]{1,0:T(8,128)(2,1)} async-done(((bf16[256,1024]{1,0:T(8,128)(2,1)}), bf16[64,1024]{1,0:T(8,128)(2,1)}) %reduce-scatter.28.cloned.1.call-update) | async-done | bytes 131088 | tf_op jit(solution)/shard_map/reduce_scatter | solution.py:39
  360.0 7.7 all_to_all.128
  369.8 21.8 %reduce-scatter.30.cloned.1.call-done = bf16[64,1024]{1,0:T(8,128)(2,1)} async-done(((bf16[256,1024]{1,0:T(8,128)(2,1)}), bf16[64,1024]{1,0:T(8,128)(2,1)}) %reduce-scatter.30.cloned.1.call-update) | async-done | bytes 131088 | tf_op jit(solution)/shard_map/reduce_scatter | solution.py:39
  393.0 6.0 collective-permute-done.5
  400.0 6.7 all_gather.61
  412.9 20.8 %reduce-scatter.32.cloned.1.call-done = bf16[64,1024]{1,0:T(8,128)(2,1)} async-done(((bf16[256,1024]{1,0:T(8,128)(2,1)}), bf16[64,1024]{1,0:T(8,128)(2,1)}) %reduce-scatter.32.cloned.1.call-update) | async-done | bytes 131088 | tf_op jit(solution)/shard_map/reduce_scatter | solution.py:39
  437.3 6.8 all_gather.62
  449.5 20.9 %reduce-scatter.34.cloned.1.call-done = bf16[64,1024]{1,0:T(8,128)(2,1)} async-done(((bf16[256,1024]{1,0:T(8,128)(2,1)}), bf16[64,1024]{1,0:T(8,128)(2,1)}) %reduce-scatter.34.cloned.1.call-update) | async-done | bytes 131088 | tf_op jit(solution)/shard_map/reduce_scatter | solution.py:39
  478.1 4.5 all-to-all-done.4
  485.0 21.7 %reduce-scatter.36.cloned.1.call-done = bf16[64,1024]{1,0:T(8,128)(2,1)} async-done(((bf16[256,1024]{1,0:T(8,128)(2,1)}), bf16[64,1024]{1,0:T(8,128)(2,1)}) %reduce-scatter.36.cloned.1.call-update) | async-done | bytes 131088 | tf_op jit(solution)/shard_map/reduce_scatter | solution.py:39
  508.1 5.9 collective-permute-done.6
  515.1 6.5 all_gather.63
  527.1 21.5 %reduce-scatter.38.cloned.1.call-done = bf16[64,1024]{1,0:T(8,128)(2,1)} async-done(((bf16[256,1024]{1,0:T(8,128)(2,1)}), bf16[64,1024]{1,0:T(8,128)(2,1)}) %reduce-scatter.38.cloned.1.call-update) | async-done | bytes 131088 | tf_op jit(solution)/shard_map/reduce_scatter | solution.py:39
  551.8 6.8 all_gather.64
  585.8 4.1 fusion.25
  597.4 5.8 fusion.24
  607.7 4.9 fusion.38
  617.6 3.3 all-to-all-start.7
  621.0 12.6 %reduce-scatter.42.cloned.1.call-done = bf16[64,1024]{1,0:T(8,128)(2,1)} async-done(((bf16[256,1024]{1,0:T(8,128)(2,1)}), bf16[64,1024]{1,0:T(8,128)(2,1)}) %reduce-scatter.42.cloned.1.call-update) | async-done | bytes 131088 | tf_op jit(solution)/shard_map/reduce_scatter | solution.py:39
  638.6 12.1 %all-reduce = (bf16[1024]{0:T(1024)(128)(2,1)S(1)}, bf16[1024]{0:T(1024)(128)(2,1)S(1)}, bf16[1024]{0:T(1024)(128)(2,1)S(1)}, bf16[1024]{0:T(1024)(128)(2,1)S(1)}) all-reduce(f32[1024]{0:T(1024)S(1)} %get-tuple-element.101, f32[1024]{0:T(1024)S(1)} %get-tuple-element.100, ...), channel_id=1, replica_groups=mesh['section'=2,'dp'=4,'tensor'=4] {'tensor'}, use_global_device_ids=true, to_apply=%region_55.56 | all-reduce | flops 4096 | bytes 24576 | tf_op jit(solution)/shard_map/psum | solution.py:292
  650.8 19.3 %all-reduce.1 = (bf16[1,1024]{1,0:T(2,128)(2,1)S(1)}, bf16[1,1024]{1,0:T(2,128)(2,1)S(1)}, bf16[1,1024]{1,0:T(2,128)(2,1)S(1)}, bf16[1,1024]{1,0:T(2,128)(2,1)S(1)}) all-reduce(bf16[1,1024]{1,0:T(2,128)(2,1)S(1)} %broadcast_in_dim.93, ...), channel_id=1, replica_groups=mesh['section'=2,'dp'=4,'tensor'=4] {'dp'}, use_global_device_ids=true, to_apply=%region_56.57 | all-reduce | flops 4096 | bytes 16384 | tf_op jit(solution)/shard_map/psum | solution.py:296
  673.1 205.6 %all-reduce.5.cloned.1.call-done = (bf16[1,1024,768]{2,1,0:T(8,128)(2,1)}, bf16[1,256,1024]{2,1,0:T(8,128)(2,1)}, bf16[1,1024,1024]{2,1,0:T(8,128)(2,1)}, bf16[1...) async-done(((bf16[1,1024,768]{2,1,0:T(8,128)(2,1)}, bf16[1,256,1024]{2,1,0:T(8,128)(2,1)}, bf16[1,1024,1024]{2,1,0:T(8,128)(2,1)}, bf16[1,1024,1024]{2,1,0:T(8,128)(2,1)}, ...) | async-done | bytes 6815760 | tf_op jit(solution)/shard_map/psum | solution.py:300
  878.7 3.5 broadcast_in_dim.102
  (517 shorter events, 187.2 us)
Async XLA Ops:
  7.2 78.4 %copy-start = (bf16[1,1024,1024]{2,1,0:T(8,128)(2,1)S(1)}, bf16[1,1024,1024]{2,1,0:T(8,128)(2,1)}, u32[]{:S(2)}) copy-start(bf16[1,1024,1024]{2,1,0:T(8,128)(2,1)} %param.21) | copy-start | bytes 6291460
  7.2 22.0 %all-gather.5.cloned.1.call-start = ((), (), s32[]{:S(2)}) async-start(), calls=%async_computation.24 | async-start | bytes 1310720 | tf_op jit(solution)/shard_map/all_gather | solution.py:219
  9.3 40.4 %copy-start.137 = (f32[4]{0:T(128)}, f32[4]{0:T(128)S(1)}, u32[]{:S(2)}) copy-start(f32[4]{0:T(128)S(1)} %multiply_power_fusion) | copy-start | bytes 52
  9.4 27.5 %copy-start.111 = (s32[256]{0:T(256)}, s32[256]{0:T(256)S(1)}, u32[]{:S(2)}) copy-start(s32[256]{0:T(256)S(1)} %fusion.245) | copy-start | bytes 3076
  31.3 8.1 all-to-all-start
  34.8 41.7 %reduce-scatter.16.cloned.1.call-start = ((), (), s32[]{:S(2)}) async-start(), calls=%async_computation.25 | async-start | bytes 655360 | tf_op jit(solution)/shard_map/reduce_scatter | solution.py:39
  39.6 36.9 %copy-start.17 = (f32[64,1024]{1,0:T(8,128)}, f32[64,1024]{1,0:T(8,128)S(1)}, u32[]{:S(2)}) copy-start(f32[64,1024]{1,0:T(8,128)S(1)} %get-tuple-element.70) | copy-start | bytes 786436
  52.2 25.5 %copy-start.86 = (f32[1,1024]{1,0:T(1,128)S(1)}, f32[1,1024]{1,0:T(1,128)}, u32[]{:S(2)}) copy-start(f32[1,1024]{1,0:T(1,128)} %param.17) | copy-start | bytes 12292
  52.2 25.5 %copy-start.92 = (f32[1,1024]{1,0:T(1,128)S(1)}, f32[1,1024]{1,0:T(1,128)}, u32[]{:S(2)}) copy-start(f32[1,1024]{1,0:T(1,128)} %param.18) | copy-start | bytes 12292
  54.0 59.2 %reduce-scatter.18.cloned.1.call-start = ((), (), s32[]{:S(2)}) async-start(), calls=%async_computation.26 | async-start | bytes 655360 | tf_op jit(solution)/shard_map/reduce_scatter | solution.py:39
  87.3 30.3 %copy-start.112 = (s32[256]{0:T(256)S(1)}, s32[256]{0:T(256)}, u32[]{:S(2)}) copy-start(s32[256]{0:T(256)} %copy-done.111) | copy-start | bytes 3076
  114.1 6.8 collective-permute-start
  118.1 9.4 %collective-permute-start.1 = (bf16[256,256]{1,0:T(8,128)(2,1)}, bf16[256,256]{1,0:T(8,128)(2,1)S(1)}, u32[]{:S(2)}, u32[]{:S(2)}) collective-permute-start(bf16[256,256]{1,0:T(8,128)(2,1)} %convolution_convert_fusion.12), channel_id=1, source_target_pairs={{0,16},{1,17},{2,18},{3,19},{4,20},{5,21},{6,22},{7,23},{8,24},{9,... | collective-permute-start | bytes 393224 | tf_op jit(solution)/shard_map/ppermute | solution.py:19
  130.5 7.9 all-to-all-start.1
  133.8 44.4 %reduce-scatter.20.cloned.1.call-start = ((), (), s32[]{:S(2)}) async-start(), calls=%async_computation.27 | async-start | bytes 655360 | tf_op jit(solution)/shard_map/reduce_scatter | solution.py:39
  139.6 38.6 %copy-start.19 = (f32[64,1024]{1,0:T(8,128)}, f32[64,1024]{1,0:T(8,128)S(1)}, u32[]{:S(2)}) copy-start(f32[64,1024]{1,0:T(8,128)S(1)} %get-tuple-element.66) | copy-start | bytes 786436
  154.7 59.9 %reduce-scatter.22.cloned.1.call-start = ((), (), s32[]{:S(2)}) async-start(), calls=%async_computation.28 | async-start | bytes 655360 | tf_op jit(solution)/shard_map/reduce_scatter | solution.py:39
  192.4 66.7 %all-gather.3.cloned.1.call-start = ((), (), s32[]{:S(2)}) async-start(), calls=%async_computation.23 | async-start | bytes 1310720 | tf_op jit(solution)/shard_map/all_gather | solution.py:220
  215.6 7.3 collective-permute-start.2
  219.0 12.1 %collective-permute-start.3 = (bf16[256,256]{1,0:T(8,128)(2,1)}, bf16[256,256]{1,0:T(8,128)(2,1)S(1)}, u32[]{:S(2)}, u32[]{:S(2)}) collective-permute-start(bf16[256,256]{1,0:T(8,128)(2,1)} %get-tuple-element.76), channel_id=1, source_target_pairs={{0,16},{1,17},{2,18},{3,19},{4,20},{5,21},{6,22},{7,23},{8,24},{9,... | collective-permute-start | bytes 393224 | tf_op jit(solution)/shard_map/ppermute | solution.py:19
  234.1 8.0 all-to-all-start.2
  237.4 45.2 %reduce-scatter.24.cloned.1.call-start = ((), (), s32[]{:S(2)}) async-start(), calls=%async_computation.29 | async-start | bytes 655360 | tf_op jit(solution)/shard_map/reduce_scatter | solution.py:39
  258.3 61.9 %reduce-scatter.26.cloned.1.call-start = ((), (), s32[]{:S(2)}) async-start(), calls=%async_computation.30 | async-start | bytes 655360 | tf_op jit(solution)/shard_map/reduce_scatter | solution.py:39
  298.0 58.9 %reduce-scatter.28.cloned.1.call-start = ((), (), s32[]{:S(2)}) async-start(), calls=%async_computation.31 | async-start | bytes 655360 | tf_op jit(solution)/shard_map/reduce_scatter | solution.py:39
  332.5 24.5 %copy-start.120 = (f32[64]{0:T(128)S(1)}, f32[64]{0:T(128)}, u32[]{:S(2)}) copy-start(f32[64]{0:T(128)} %copy-done.119) | copy-start | bytes 772
  332.5 24.5 %copy-start.128 = (f32[64]{0:T(128)S(1)}, f32[64]{0:T(128)}, u32[]{:S(2)}) copy-start(f32[64]{0:T(128)} %copy-done.127) | copy-start | bytes 772
  334.7 58.2 %copy-start.132 = (f32[256]{0:T(256)S(1)}, f32[256]{0:T(256)}, u32[]{:S(2)}) copy-start(f32[256]{0:T(256)} %get-tuple-element.55) | copy-start | bytes 3076
  334.8 56.9 %reduce-scatter.30.cloned.1.call-start = ((), (), s32[]{:S(2)}) async-start(), calls=%async_computation.32 | async-start | bytes 655360 | tf_op jit(solution)/shard_map/reduce_scatter | solution.py:39
  369.8 63.8 %reduce-scatter.32.cloned.1.call-start = ((), (), s32[]{:S(2)}) async-start(), calls=%async_computation.33 | async-start | bytes 655360 | tf_op jit(solution)/shard_map/reduce_scatter | solution.py:39
  391.6 7.3 collective-permute-start.5
  412.1 58.3 %reduce-scatter.34.cloned.1.call-start = ((), (), s32[]{:S(2)}) async-start(), calls=%async_computation.34 | async-start | bytes 655360 | tf_op jit(solution)/shard_map/reduce_scatter | solution.py:39
  445.9 24.5 %copy-start.117 = (f32[64]{0:T(128)S(1)}, f32[64]{0:T(128)}, u32[]{:S(2)}) copy-start(f32[64]{0:T(128)} %copy-done.116) | copy-start | bytes 772
  445.9 24.5 %copy-start.125 = (f32[64]{0:T(128)S(1)}, f32[64]{0:T(128)}, u32[]{:S(2)}) copy-start(f32[64]{0:T(128)} %copy-done.124) | copy-start | bytes 772
  448.2 59.8 %copy-start.131 = (f32[256]{0:T(256)S(1)}, f32[256]{0:T(256)}, u32[]{:S(2)}) copy-start(f32[256]{0:T(256)} %get-tuple-element.77) | copy-start | bytes 3076
  448.2 29.9 %collective-permute-start.4 = (bf16[256,256]{1,0:T(8,128)(2,1)}, bf16[256,256]{1,0:T(8,128)(2,1)}, u32[]{:S(2)}, u32[]{:S(2)}) collective-permute-start(bf16[256,256]{1,0:T(8,128)(2,1)} %bitcast.52), channel_id=1, source_target_pairs={{16,0},{17,1},{18,2},{19,3},{20,4},{21,5},{22,6},{23,7},{24,8},{25... | collective-permute-start | bytes 393224 | tf_op jit(solution)/shard_map/ppermute | solution.py:19
  474.7 7.9 all-to-all-start.4
  478.1 28.6 %reduce-scatter.36.cloned.1.call-start = ((), (), s32[]{:S(2)}) async-start(), calls=%async_computation.35 | async-start | bytes 655360 | tf_op jit(solution)/shard_map/reduce_scatter | solution.py:39
  484.9 63.7 %reduce-scatter.38.cloned.1.call-start = ((), (), s32[]{:S(2)}) async-start(), calls=%async_computation.36 | async-start | bytes 655360 | tf_op jit(solution)/shard_map/reduce_scatter | solution.py:39
  506.7 7.3 collective-permute-start.6
  527.0 31.9 %copy-start.4 = (f32[4,256,256]{1,2,0:T(8,128)S(1)}, f32[4,256,256]{1,2,0:T(8,128)}, u32[]{:S(2)}) copy-start(f32[4,256,256]{1,2,0:T(8,128)} %copy-done.3) | copy-start | bytes 3145732
  527.1 62.8 %reduce-scatter.40.cloned.1.call-start = ((), (), s32[]{:S(2)}) async-start(), calls=%async_computation.37 | async-start | bytes 655360 | tf_op jit(solution)/shard_map/reduce_scatter | solution.py:39
  562.7 52.5 %reduce-scatter.44.cloned.1.call-start = ((), (), s32[]{:S(2)}) async-start(), calls=%async_computation.39 | async-start | bytes 655360 | tf_op jit(solution)/shard_map/reduce_scatter | solution.py:39
  582.0 21.2 %collective-permute-start.7 = (bf16[256,256]{1,0:T(8,128)(2,1)S(1)}, bf16[256,256]{1,0:T(8,128)(2,1)}, u32[]{:S(2)}, u32[]{:S(2)}) collective-permute-start(bf16[256,256]{1,0:T(8,128)(2,1)S(1)} %bitcast.434), channel_id=1, source_target_pairs={{16,0},{17,1},{18,2},{19,3},{20,4},{21,5},{22,6},{23,7},{24,8},{25... | collective-permute-start | bytes 393224 | tf_op jit(solution)/shard_map/ppermute | solution.py:19
  594.0 9.2 %all-to-all-start.5 = ((bf16[64,4,256]{2,0,1:T(8,128)(2,1)}), bf16[64,4,256]{2,0,1:T(8,128)(2,1)S(1)}, u32[]{:S(2)}, u32[]{:S(2)}) async-start(bf16[64,4,256]{2,0,1:T(8,128)(2,1)} %bitcast.403), calls=%async_computation.18 | async-start | bytes 262144 | tf_op jit(solution)/shard_map/all_to_all | solution.py:60
  597.4 36.3 %reduce-scatter.42.cloned.1.call-start = ((), (), s32[]{:S(2)}) async-start(), calls=%async_computation.38 | async-start | bytes 655360 | tf_op jit(solution)/shard_map/reduce_scatter | solution.py:39
  605.3 273.4 %all-reduce.5.cloned.1.call-start = ((), (), s32[]{:S(2)}) async-start(), calls=%async_computation.40 | async-start | bytes 13631488 | tf_op jit(solution)/shard_map/psum | solution.py:300
  617.6 17.6 %all-to-all-start.7 = ((bf16[64,4,256]{2,0,1:T(8,128)(2,1)}), bf16[64,4,256]{2,0,1:T(8,128)(2,1)S(1)}, u32[]{:S(2)}, u32[]{:S(2)}) async-start(bf16[64,4,256]{2,0,1:T(8,128)(2,1)} %bitcast.401), calls=%async_computation.22 | async-start | bytes 262144 | tf_op jit(solution)/shard_map/all_to_all | solution.py:60
  635.2 37.2 %all-to-all-start.6 = ((bf16[64,4,256]{2,0,1:T(8,128)(2,1)}), bf16[64,4,256]{2,0,1:T(8,128)(2,1)S(1)}, u32[]{:S(2)}, u32[]{:S(2)}) async-start(bf16[64,4,256]{2,0,1:T(8,128)(2,1)} %bitcast.402), calls=%async_computation.20 | async-start | bytes 262144 | tf_op jit(solution)/shard_map/all_to_all | solution.py:60
  (124 other events, 620.2 us)
Sparse Core Ops, SparseCore 0:
  9.6 19.5 all-gather.4
  54.1 22.2 reduce-scatter.15
  91.1 22.0 reduce-scatter.17
  154.8 23.3 reduce-scatter.19
  192.6 22.0 reduce-scatter.21
  219.1 16.7 all-gather.2
  258.4 24.2 reduce-scatter.23
  298.1 22.0 reduce-scatter.25
  334.9 22.0 reduce-scatter.27
  369.9 21.6 reduce-scatter.29
  412.2 21.3 reduce-scatter.31
  448.3 22.0 reduce-scatter.33
  485.0 21.6 reduce-scatter.35
  527.2 21.3 reduce-scatter.37
  562.8 21.9 reduce-scatter.39
  587.3 21.6 reduce-scatter.43
  611.9 21.6 reduce-scatter.41
  637.0 241.6 all-reduce.4
where the time goes:
time: 907 us; the launch traced here: 897 us
  waiting for transfers between devices  523 us (58%)
  blocking collectives  135 us (15%)
  matrix products  97.5 us (11%)
  other arithmetic  55.1 us (6%)
  starting transfers between devices  39 us (4%)
  local copies, waits for them, and re-layouts  30.7 us (3%)
  between operations  16.4 us (2%)
    reduce_scatter x15, waiting for transfers between devices, reduce_rows(): lax.psum_scatter(partial_sum.astype(jnp.bfloat16), 'tensor', scatter_dime...  266 us
    psum x1, waiting for transfers between devices, shards(): lax.psum(qkv_total.astype(jnp.bfloat16), 'dp').astype(jnp.float32)  206 us
    all_gather x14, blocking collectives, whole_rows(): return lax.all_gather(rounded, 'tensor', axis=0, tiled=True)  96.2 us
    dot_general x15, matrix products, product_tn(): lax.dot_general(left, right, (((0,), (0,)), ((), ())), preferred_element_...  35.9 us
    dot_general x15, matrix products, product(): return jnp.dot(left, right, preferred_element_type=jnp.float32)  30.4 us
    dot_general x15, matrix products, product_nt(): lax.dot_general(left, right, (((1,), (1,)), ((), ())), preferred_element_...  21.4 us
    psum x1, blocking collectives, shards(): lax.psum(gain_one.astype(jnp.bfloat16), 'dp').astype(jnp.float32)  19.3 us
    all_gather x1, waiting for transfers between devices, shards(): lax.all_gather(frames, 'tensor', axis=2, tiled=True)  18.3 us
  transfers between devices with their start and end apart: 33, of which 23 were waited for; matrix products, arithmetic and copies ran while one was open for 8% of the time, Pallas kernels for 0%

commit v1 on v0

v1 whole, which is shorter than its diff:
```python
import functools

import jax
import jax.numpy as jnp
from jax import lax
from jax.experimental import pallas as pl
from jax.experimental.pallas import tpu as pltpu
from jax.sharding import PartitionSpec as P

HEADS = 16
HD = 64
UTT = 2

epsilon = 1e-05
inv_root_two = 0.7071067811865476
inv_root_two_pi = 0.3989422804014327
MIB = 1 << 20
GROUP = 4


def core_swap(value):
    count = lax.axis_size("tensor")
    return lax.ppermute(value, "tensor", [(at, at ^ 1) for at in range(count)])


def x_swap(value):
    count = lax.axis_size("tensor")
    return lax.ppermute(value, "tensor", [(at, at ^ 2) for at in range(count)])


def section_swap(value):
    return lax.ppermute(value, "section", [(0, 1), (1, 0)])


def dp_swap(value, bit):
    count = lax.axis_size("dp")
    return lax.ppermute(value, "dp", [(at, at ^ bit) for at in range(count)])


def dp_shift(value, steps):
    count = lax.axis_size("dp")
    return lax.ppermute(value, "dp", [(at, (at + steps) % count) for at in range(count)])


def sum_half(theirs, mine):
    near = (mine.astype(jnp.float32) + core_swap(theirs).astype(jnp.float32)).astype(jnp.bfloat16)
    return near, x_swap(near)


def sum_whole(theirs, mine):
    near, far = sum_half(theirs, mine)
    half = (near.astype(jnp.float32) + far.astype(jnp.float32)).astype(jnp.bfloat16)
    return half, core_swap(half)


def dot(left, right):
    return jnp.dot(left, right, preferred_element_type=jnp.float32)


def dot_nt(left, right):
    return lax.dot_general(
        left, right, (((1,), (1,)), ((), ())), preferred_element_type=jnp.float32
    )


def dot_tn(left, right):
    return lax.dot_general(
        left, right, (((0,), (0,)), ((), ())), preferred_element_type=jnp.float32
    )


def f32(ref):
    return ref[...].astype(jnp.float32)


def both(mine, other):
    return jnp.concatenate([f32(mine), f32(other)], 0)


def norm_stats(inputs):
    average = jnp.mean(inputs, -1, keepdims=True)
    centred = inputs - average
    inverse = lax.rsqrt(jnp.mean(centred * centred, -1, keepdims=True) + epsilon)
    return centred * inverse, inverse


def norm_back(grad_norm, normed, inverse, gain):
    scaled = grad_norm * gain
    return inverse * (
        scaled
        - jnp.mean(scaled, -1, keepdims=True)
        - normed * jnp.mean(scaled * normed, -1, keepdims=True)
    )


def erf(value):
    value = jnp.clip(value, -3.832506856900711, 3.832506856900711)
    square = value * value
    top = 0.00022905065861350646
    for term in (
        0.0034082910107109506,
        0.050955695062380861,
        0.18520832239976145,
        1.128379143519084,
    ):
        top = top * square + term
    below = -1.1791602954361697e-7
    for term in (
        0.000023547966471313185,
        0.0010179625278914885,
        0.014070470171167667,
        0.11098505178285362,
        0.49746925110067538,
        1.0,
    ):
        below = below * square + term
    return value * top / below


def gelu_and_slope(hidden):
    normal_cdf = 0.5 * (1.0 + erf(hidden * inv_root_two))
    normal_pdf = jnp.exp(-0.5 * hidden * hidden) * inv_root_two_pi
    return hidden * normal_cdf, normal_cdf + hidden * normal_pdf


def pair_masks(turn, first_len, second_len, rows):
    def place(axis):
        at = lax.broadcasted_iota(jnp.int32, (rows, rows), axis) + turn
        return jnp.where(at >= rows, at - rows, at)

    def segment(at):
        return (at >= first_len).astype(jnp.int32) + (at >= first_len + second_len).astype(
            jnp.int32
        )

    queries, keys_all = place(0), place(1)
    return (
        segment(queries) == segment(keys_all),
        jnp.abs(queries - keys_all).astype(jnp.float32),
    )


def head_columns(rows, heads, head):
    lane = lax.broadcasted_iota(jnp.int32, (rows, heads * HD), 1)
    return (lane >= head * HD) & (lane < (head + 1) * HD)


def keep(mask, value):
    return jnp.where(mask, value, jnp.zeros_like(value))


def attention_probs(packed, slopes, allowed, distance, head, heads):
    rows, wide = packed.shape[0], heads * HD
    mask = head_columns(rows, heads, head)
    scores = dot_nt(keep(mask, packed[:, :wide]), packed[:, wide : 2 * wide]) * HD ** (-0.5)
    scores = jnp.where(allowed, scores - slopes[head] * distance, -1e30)
    exp_scores = jnp.exp(scores - jnp.max(scores, -1, keepdims=True))
    return (exp_scores / jnp.sum(exp_scores, -1, keepdims=True)).astype(jnp.bfloat16)


def attention_back(packed, grad_mix, probs_of, heads):
    rows, wide = packed.shape[0], heads * HD
    queries, keys_all, values = packed[:, :wide], packed[:, wide : 2 * wide], packed[:, 2 * wide :]
    grads = [jnp.zeros((rows, wide), jnp.float32) for _ in range(3)]
    for head in range(heads):
        mask = head_columns(rows, heads, head)
        probs = probs_of(head)
        grad_here = keep(mask, grad_mix)
        grad_probs = dot_nt(grad_here, values)
        wide_probs = probs.astype(jnp.float32)
        row_delta = jnp.sum(wide_probs * grad_probs, -1, keepdims=True)
        grad_scores = (wide_probs * (grad_probs - row_delta)).astype(jnp.bfloat16)
        grads[0] += dot(grad_scores, keep(mask, keys_all))
        grads[1] += dot_tn(grad_scores, keep(mask, queries))
        grads[2] += dot_tn(probs, grad_here)
    scale = HD ** (-0.5)
    return jnp.concatenate([grads[0] * scale, grads[1] * scale, grads[2]], 1).astype(jnp.bfloat16)


def store_halves(partial_sum, theirs, mine):
    half = mine.shape[0]
    mine[...] = partial_sum[:half].astype(mine.dtype)
    theirs[...] = partial_sum[half:].astype(theirs.dtype)


def attn_fwd_kernel(
    meta, slopes, v_mine, v_other, gain, bias, w_qkv, w_out, a_mine, packed_out, probs_out, theirs, mine
):
    heads, rows, _ = probs_out.shape
    normed, _ = norm_stats(both(v_mine, v_other))
    attn_in = (normed * gain[...] + bias[...]).astype(jnp.bfloat16)
    a_mine[...] = attn_in[: a_mine.shape[0]]
    packed = dot(attn_in, w_qkv[...]).astype(jnp.bfloat16)
    packed_out[...] = packed
    allowed, distance = pair_masks(meta[0] * a_mine.shape[0], meta[1], meta[2], rows)
    head_mix = jnp.zeros((rows, heads * HD), jnp.float32)
    for head in range(heads):
        probs = attention_probs(packed, slopes, allowed, distance, head, heads)
        probs_out[head] = probs
        values = keep(head_columns(rows, heads, head), packed[:, 2 * heads * HD :])
        head_mix += dot(probs, values)
    store_halves(dot(head_mix.astype(jnp.bfloat16), w_out[...]), theirs, mine)


def ffn_fwd_kernel(
    v_mine, v_other, s_mine, s_other, gain, bias, w_up, w_down,
    c_mine, x1_mine, slope_out, theirs, mine, ffn_in, total,
):
    step = pl.program_id(0)

    @pl.when(step == 0)
    def _():
        middle = both(v_mine, v_other) + both(s_mine, s_other)
        x1_mine[...] = middle[: x1_mine.shape[0]]
        normed, _ = norm_stats(middle)
        rounded = (normed * gain[...] + bias[...]).astype(jnp.bfloat16)
        ffn_in[...] = rounded
        c_mine[...] = rounded[: c_mine.shape[0]]
        total[...] = jnp.zeros_like(total)

    activated, act_slope = gelu_and_slope(dot(ffn_in[...], w_up[...]))
    slope_out[...] = act_slope
    total[...] += dot(activated.astype(jnp.bfloat16), w_down[...])

    @pl.when(step == pl.num_programs(0) - 1)
    def _():
        store_halves(total[...], theirs, mine)


def ffn_back_kernel(g_mine, g_other, slope_in, w_down, w_up, theirs, mine, total):
    step = pl.program_id(0)

    @pl.when(step == 0)
    def _():
        total[...] = jnp.zeros_like(total)

    grad = jnp.concatenate([g_mine[...], g_other[...]], 0)
    grad_pre = (dot_nt(grad, w_down[...]) * slope_in[...]).astype(jnp.bfloat16)
    total[...] += dot_nt(grad_pre, w_up[...])

    @pl.when(step == pl.num_programs(0) - 1)
    def _():
        store_halves(total[...], theirs, mine)


def attn_back_kernel(
    g_mine, g_other, v_mine, v_other, s_mine, s_other, t_mine, t_other, gain, w_out, w_qkv, packed, probs,
    ga_mine, x1_grad_mine, norm_grads, theirs, mine,
):
    heads = probs.shape[0]
    half = ga_mine.shape[0]
    normed, inverse = norm_stats(both(v_mine, v_other) + both(s_mine, s_other))
    grad_norm = both(t_mine, t_other)
    grad_mid = both(g_mine, g_other) + norm_back(grad_norm, normed, inverse, gain[...])
    x1_grad_mine[...] = grad_mid[:half]
    norm_grads[0:1] = jnp.sum(grad_norm[:half] * normed[:half], 0, keepdims=True)
    norm_grads[1:2] = jnp.sum(grad_norm[:half], 0, keepdims=True)
    grad_attn = grad_mid.astype(jnp.bfloat16)
    ga_mine[...] = grad_attn[:half]
    grad_mix = dot_nt(grad_attn, w_out[...]).astype(jnp.bfloat16)
    grad_packed = attention_back(packed[...], grad_mix, lambda head: probs[head], heads)
    store_halves(dot_nt(grad_packed, w_qkv[...]), theirs, mine)


def input_back(near, far, v_mine, x1_grad_mine, gain, norm_grads):
    normed, inverse = norm_stats(f32(v_mine))
    grad_norm = f32(near) + f32(far)
    norm_grads[0:1] = jnp.sum(grad_norm * normed, 0, keepdims=True)
    norm_grads[1:2] = jnp.sum(grad_norm, 0, keepdims=True)
    return x1_grad_mine[...] + norm_back(grad_norm, normed, inverse, gain[...])


def skip_back(rows, w_all):
    parts, _, wide = w_all.shape
    out = dot_nt(rows[:, :wide], w_all[0])
    for at in range(1, parts):
        out += dot_nt(rows[:, at * wide : (at + 1) * wide], w_all[at])
    return out


def hop_back_kernel(near, far, v_mine, x1_grad_mine, gain, w_all, joined_grad, h_grad, norm_grads):
    rounded = input_back(near, far, v_mine, x1_grad_mine, gain, norm_grads).astype(jnp.bfloat16)
    joined_grad[...] = rounded
    h_grad[...] = skip_back(rounded, w_all).astype(h_grad.dtype)


def frames_back_kernel(near, far, v_mine, x1_grad_mine, gain, w_all, joined_grad, out, norm_grads):
    grad_in = input_back(near, far, v_mine, x1_grad_mine, gain, norm_grads)
    out[...] = (grad_in + skip_back(joined_grad[...], w_all)).astype(out.dtype)


def skip_kernel(rows, w_all, out):
    wide = w_all.shape[2]
    for at in range(w_all.shape[0]):
        out[:, at * wide : (at + 1) * wide] = dot(rows[...], w_all[at]).astype(out.dtype)


def join_kernel(rows, w_all, skip_part, out):
    wide = w_all.shape[2]
    for at in range(w_all.shape[0]):
        columns = slice(at * wide, (at + 1) * wide)
        product = dot(rows[...], w_all[at]) + skip_part[:, columns].astype(jnp.float32)
        out[:, columns] = product.astype(out.dtype)


def ffn_weights_kernel(ffn_in, grad_out, w_up, w_down, grad_up, grad_down):
    @pl.when(pl.program_id(0) == 0)
    def _():
        grad_up[...] = jnp.zeros_like(grad_up)
        grad_down[...] = jnp.zeros_like(grad_down)

    wide = 256
    for at in range(0, w_up.shape[1], wide):
        units = slice(at, at + wide)
        activated, act_slope = gelu_and_slope(dot(ffn_in[...], w_up[:, units]))
        grad_pre = (dot_nt(grad_out[...], w_down[units]) * act_slope).astype(jnp.bfloat16)
        grad_down[units] += dot_tn(activated.astype(jnp.bfloat16), grad_out[...])
        grad_up[:, units] += dot_tn(ffn_in[...], grad_pre)


def attn_weights_kernel(
    here, lens, slopes, attn_in, grad_attn, w_qkv, w_out, order, grad_qkv, grad_out
):
    block = pl.program_id(0)

    @pl.when(block == 0)
    def _():
        grad_qkv[...] = jnp.zeros_like(grad_qkv)
        grad_out[...] = jnp.zeros_like(grad_out)

    heads = w_out.shape[0] // HD
    rows = attn_in.shape[0]
    per_index = here[1]
    group = here[2]
    away = lax.rem(here[0] - block // per_index + group, group)
    at = (away * per_index + lax.rem(block, per_index)) * UTT
    allowed, distance = pair_masks(0, lens[at], lens[at + 1], rows)
    packed = dot(attn_in[...], w_qkv[...]).astype(jnp.bfloat16)
    grad_mix = dot_nt(grad_attn[...], w_out[...]).astype(jnp.bfloat16)
    kept, head_mix = [], jnp.zeros((rows, heads * HD), jnp.float32)
    for head in range(heads):
        probs = attention_probs(packed, slopes, allowed, distance, head, heads)
        values = keep(head_columns(rows, heads, head), packed[:, 2 * heads * HD :])
        head_mix += dot(probs, values)
        kept.append(probs)
    grad_packed = attention_back(packed, grad_mix, lambda head: kept[head], heads)
    grad_packed = dot(grad_packed, order[...]).astype(jnp.bfloat16)
    grad_qkv[...] += dot_tn(attn_in[...], grad_packed)
    grad_out[...] += dot_tn(head_mix.astype(jnp.bfloat16), grad_attn[...])


def shape(dims, kind=jnp.bfloat16):
    return jax.ShapeDtypeStruct(dims, kind)


WHOLE = pl.BlockSpec(memory_space=pltpu.VMEM)
SCALARS = pl.BlockSpec(memory_space=pltpu.SMEM)


def call(kernel, outs, scalars, arrays, flops):
    moved = sum(item.size * item.dtype.itemsize for item in list(arrays) + list(outs))
    return pl.pallas_call(
        kernel,
        out_shape=list(outs),
        in_specs=[SCALARS] * len(scalars) + [WHOLE] * len(arrays),
        out_specs=[WHOLE] * len(outs),
        compiler_params=pltpu.CompilerParams(vmem_limit_bytes=32 * MIB),
        cost_estimate=pl.CostEstimate(flops=int(flops), bytes_accessed=int(moved), transcendentals=0),
    )(*scalars, *arrays)


def attn_forward(meta, slopes, v_mine, v_other, gain, bias, w_qkv, w_out):
    half, width = v_mine.shape
    rows, wide = 2 * half, w_out.shape[0]
    heads = wide // HD
    return call(
        attn_fwd_kernel,
        [
            shape((half, width)),
            shape((rows, 3 * wide)),
            shape((heads, rows, rows)),
            shape((half, width)),
            shape((half, width)),
        ],
        [meta, slopes],
        [v_mine, v_other, gain, bias, w_qkv, w_out],
        2 * rows * wide * (4 * width + 8 * rows),
    )


def constant(dims):
    return pl.BlockSpec(dims, lambda step: (0,) * len(dims))


def ffn_forward(v_mine, v_other, s_mine, s_other, gain, bias, w_up, w_down):
    half, width = v_mine.shape
    rows, units = 2 * half, w_up.shape[1]
    wide = min(256, units)
    part = constant((half, width))
    row = constant((1, width))
    return pl.pallas_call(
        ffn_fwd_kernel,
        grid=(units // wide,),
        in_specs=[
            part, part, part, part, row, row,
            pl.BlockSpec((width, wide), lambda step: (0, step)),
            pl.BlockSpec((wide, width), lambda step: (step, 0)),
        ],
        out_specs=[part, part, pl.BlockSpec((rows, wide), lambda step: (0, step)), part, part],
        out_shape=[
            shape((half, width)),
            shape((half, width), jnp.float32),
            shape((rows, units), jnp.float32),
            shape((half, width)),
            shape((half, width)),
        ],
        scratch_shapes=[pltpu.VMEM((rows, width), jnp.bfloat16), pltpu.VMEM((rows, width), jnp.float32)],
        compiler_params=pltpu.CompilerParams(vmem_limit_bytes=32 * MIB),
        cost_estimate=pl.CostEstimate(
            flops=4 * rows * width * units, bytes_accessed=4 * width * units + 4 * rows * units, transcendentals=0
        ),
    )(v_mine, v_other, s_mine, s_other, gain, bias, w_up, w_down)


def ffn_backward(g_mine, g_other, slope, w_down, w_up):
    half, width = g_mine.shape
    rows, units = 2 * half, w_up.shape[1]
    wide = min(256, units)
    part = constant((half, width))
    return pl.pallas_call(
        ffn_back_kernel,
        grid=(units // wide,),
        in_specs=[
            part, part,
            pl.BlockSpec((rows, wide), lambda step: (0, step)),
            pl.BlockSpec((wide, width), lambda step: (step, 0)),
            pl.BlockSpec((width, wide), lambda step: (0, step)),
        ],
        out_specs=[part, part],
        out_shape=[shape((half, width)), shape((half, width))],
        scratch_shapes=[pltpu.VMEM((rows, width), jnp.float32)],
        compiler_params=pltpu.CompilerParams(vmem_limit_bytes=32 * MIB),
        cost_estimate=pl.CostEstimate(
            flops=4 * rows * width * units, bytes_accessed=4 * width * units + 4 * rows * units, transcendentals=0
        ),
    )(g_mine, g_other, slope, w_down, w_up)


def attn_backward(g, v, s, t, gain, w_out, w_qkv, packed, probs):
    half, width = g[0].shape
    rows, wide = 2 * half, w_out.shape[0]
    return call(
        attn_back_kernel,
        [
            shape((half, width)),
            shape((half, width), jnp.float32),
            shape((2, width), jnp.float32),
            shape((half, width)),
            shape((half, width)),
        ],
        [],
        [*g, *v, *s, *t, gain, w_out, w_qkv, packed, probs],
        2 * rows * wide * (4 * width + 16 * rows),
    )


def ffn_weights(ffn_in, grad_out, w_up, w_down, block):
    width, units = w_up.shape
    rows = ffn_in.shape[0]
    piece = pl.BlockSpec((block, width), lambda step: (step, 0))
    return pl.pallas_call(
        ffn_weights_kernel,
        grid=(rows // block,),
        in_specs=[piece, piece, constant((width, units)), constant((units, width))],
        out_specs=[constant((width, units)), constant((units, width))],
        out_shape=[shape((width, units), jnp.float32), shape((units, width), jnp.float32)],
        compiler_params=pltpu.CompilerParams(vmem_limit_bytes=52 * MIB),
        cost_estimate=pl.CostEstimate(
            flops=8 * rows * width * units, bytes_accessed=16 * width * units, transcendentals=0
        ),
    )(ffn_in, grad_out, w_up, w_down)


def attn_weights(here, lens, slopes, attn_in, grad_attn, w_qkv, w_out, order, block):
    wide, width = w_out.shape
    rows = attn_in.shape[0]
    piece = pl.BlockSpec((block, width), lambda step: (step, 0))
    return pl.pallas_call(
        attn_weights_kernel,
        grid=(rows // block,),
        in_specs=[
            SCALARS, SCALARS, SCALARS, piece, piece,
            constant((width, 3 * wide)), constant((wide, width)), constant((3 * wide, 3 * wide)),
        ],
        out_specs=[constant((width, 3 * wide)), constant((wide, width))],
        out_shape=[shape((width, 3 * wide), jnp.float32), shape((wide, width), jnp.float32)],
        compiler_params=pltpu.CompilerParams(vmem_limit_bytes=48 * MIB),
        cost_estimate=pl.CostEstimate(
            flops=2 * rows * wide * (8 * width + 24 * block), bytes_accessed=24 * width * wide, transcendentals=0
        ),
    )(here, lens, slopes, attn_in, grad_attn, w_qkv, w_out, order)


def shards(
    frames,
    cotangent,
    lengths,
    norm1_gain,
    norm1_bias,
    norm2_gain,
    norm2_bias,
    w_qkv,
    w_out,
    w_up,
    w_down,
    w_skip,
):
    first = lax.axis_index("section") == 0
    dp_at = lax.axis_index("dp")
    tensor_at = lax.axis_index("tensor")
    core, chip = tensor_at % 2, tensor_at // 2
    dp_count = lax.axis_size("dp")
    micro, rows, quarter = frames.shape
    half = rows // 2
    w_qkv, w_out, w_up, w_down = w_qkv[0], w_out[0], w_up[0], w_down[0]
    heads = w_qkv.shape[1] // (3 * HD)
    wide = heads * HD

    def halves(whole):
        return (
            lax.dynamic_slice_in_dim(whole, core * half, half, 0),
            lax.dynamic_slice_in_dim(whole, (1 - core) * half, half, 0),
        )

    at = jnp.arange(3 * wide, dtype=jnp.int32)
    source = (at % wide) // HD * (3 * HD) + at // wide * HD + at % HD
    order = (source[:, None] == at[None, :]).astype(jnp.bfloat16)
    w_packed = dot_nt(w_qkv, order).astype(jnp.bfloat16)

    head_ids = tensor_at * heads + jnp.arange(heads, dtype=jnp.int32)
    slopes = 2.0 ** (-8.0 * (head_ids + 1).astype(jnp.float32) / HEADS)
    metas = [
        jnp.concatenate([core[None].astype(jnp.int32), lengths[m, 0]]) for m in range(micro)
    ]

    xs = [halves(lax.all_gather(frames[m], "tensor", axis=1, tiled=True)) for m in range(micro)]
    w_all = lax.all_gather(w_skip[0], "tensor", axis=0, tiled=False)
    whole_cot = lax.all_gather(cotangent, "tensor", axis=2, tiled=True)

    gather_dp = dp_count <= GROUP
    group = dp_count if gather_dp else 1
    lens = [lengths.reshape(-1)]
    for steps in range(1, group):
        lens.append(dp_shift(lens[0], steps))
    lens = jnp.concatenate(lens)
    here = jnp.stack([dp_at % group, jnp.int32(micro), jnp.int32(group)]).astype(jnp.int32)

    def forward(v):
        attn = [
            attn_forward(metas[m], slopes, *v[m], norm1_gain, norm1_bias, w_packed, w_out)
            for m in range(micro)
        ]
        sums = [sum_whole(item[3], item[4]) for item in attn]
        ffn = [
            ffn_forward(*v[m], *sums[m], norm2_gain, norm2_bias, w_up, w_down)
            for m in range(micro)
        ]
        outs = []
        for item in ffn:
            near, far = sum_half(item[3], item[4])
            outs.append((item[1] + near.astype(jnp.float32) + far.astype(jnp.float32)).astype(jnp.bfloat16))
        kept = dict(
            v=v,
            sums=sums,
            packed=[item[1] for item in attn],
            probs=[item[2] for item in attn],
            slope=[item[2] for item in ffn],
            attn_in=[item[0] for item in attn],
            ffn_in=[item[0] for item in ffn],
        )
        return outs, kept

    def backward(g, kept):
        ffn = [ffn_backward(*g[m], kept["slope"][m], w_down, w_up) for m in range(micro)]
        sums = [sum_whole(*item) for item in ffn]
        attn = [
            attn_backward(
                g[m], kept["v"][m], kept["sums"][m], sums[m], norm2_gain, w_out, w_packed,
                kept["packed"][m], kept["probs"][m],
            )
            for m in range(micro)
        ]
        halves_in = [sum_half(item[3], item[4]) for item in attn]
        return attn, halves_in

    skip_parts = [
        section_swap(call(skip_kernel, [shape(v[0].shape)], [], [v[0], w_all], 2 * v[0].size * v[0].shape[1])[0])
        for v in xs
    ]
    outs_a, kept_a = forward(xs)
    h_recv = [section_swap(item) for item in outs_a]
    joined = []
    for m in range(micro):
        mine = call(
            join_kernel, [shape(h_recv[m].shape)], [], [h_recv[m], w_all, skip_parts[m]], 2 * h_recv[m].size * h_recv[m].shape[1]
        )[0]
        joined.append((mine, core_swap(mine)))
    outs_b, kept_b = forward(joined)

    positions = jnp.arange(rows, dtype=jnp.int32)
    g_c = []
    for m in range(micro):
        valid = (positions < jnp.sum(lengths[m, 0]))[:, None]
        g_c.append(halves(jnp.where(valid, whole_cot[m], jnp.zeros_like(whole_cot[m]))))
    attn_c, sums_c = backward(g_c, kept_b)
    half_dims = shape((half, norm1_gain.shape[1]))
    vector = shape((2, norm1_gain.shape[1]), jnp.float32)
    square = 2 * half * norm1_gain.shape[1] ** 2
    hop = [
        call(
            hop_back_kernel, [half_dims, half_dims, vector], [],
            [*sums_c[m], kept_b["v"][m][0], attn_c[m][1], norm1_gain, w_all], square,
        )
        for m in range(micro)
    ]
    g_d = []
    for m in range(micro):
        mine = section_swap(hop[m][1])
        g_d.append((mine, core_swap(mine)))
    joined_recv = [section_swap(item[0]) for item in hop]
    attn_d, sums_d = backward(g_d, kept_a)
    last = [
        call(
            frames_back_kernel, [half_dims, vector], [],
            [*sums_d[m], kept_a["v"][m][0], attn_d[m][1], norm1_gain, w_all, joined_recv[m]], square,
        )
        for m in range(micro)
    ]

    def choose(early, late):
        return jnp.where(first, early, late)

    def all_rows(early, late):
        mine = jnp.where(
            chip == 0, choose(early[0], late[0]), choose(early[1], late[1])
        )
        if gather_dp:
            return lax.all_gather(mine, ("dp", "tensor"), axis=0, tiled=True)
        return lax.all_gather(mine, "tensor", axis=0, tiled=True)

    attn_in = all_rows(kept_a["attn_in"], kept_b["attn_in"])
    ffn_in = all_rows(kept_a["ffn_in"], kept_b["ffn_in"])
    grad_out = all_rows([item[0] for item in g_d], [item[0] for item in g_c])
    grad_attn = all_rows([item[0] for item in attn_d], [item[0] for item in attn_c])
    up_total, down_total = ffn_weights(ffn_in, grad_out, w_up, w_down, micro * rows)
    qkv_total, out_total = attn_weights(
        here, lens, slopes, attn_in, grad_attn, w_packed, w_out, order, rows
    )

    def over_dp(total):
        return lax.psum(total.astype(jnp.bfloat16), "dp").astype(jnp.float32)

    if not gather_dp:
        up_total, down_total, qkv_total, out_total = (
            over_dp(item) for item in (up_total, down_total, qkv_total, out_total)
        )

    def own_columns(item):
        return lax.dynamic_slice_in_dim(item, tensor_at * quarter, quarter, 1)

    def other_columns(item):
        return lax.dynamic_slice_in_dim(item, (tensor_at ^ 1) * quarter, quarter, 1)

    inputs, grads = [], []
    for m in range(micro):
        mine = choose(xs[m][0], h_recv[m])
        inputs += [mine, core_swap(mine)]
        grad = choose(joined_recv[m], hop[m][0])
        grads += [own_columns(grad), core_swap(other_columns(grad))]
    skip_total = over_dp(dot_tn(jnp.concatenate(inputs, 0), jnp.concatenate(grads, 0)))

    norm_grads = choose(
        jnp.concatenate([sum(item[1] for item in last), sum(item[2] for item in attn_d)], 0),
        jnp.concatenate([sum(item[2] for item in hop), sum(item[2] for item in attn_c)], 0),
    )
    norm_grads += core_swap(norm_grads)
    bit = 1
    while bit < dp_count:
        norm_grads += dp_swap(norm_grads, bit)
        bit *= 2

    pieces = []
    for m in range(micro):
        mine = choose(last[m][0], outs_b[m])
        own, other = own_columns(mine), core_swap(other_columns(mine))
        pieces.append(
            jnp.where(core == 0, jnp.concatenate([own, other], 0), jnp.concatenate([other, own], 0))
        )
    return (
        jnp.stack(pieces, 0)[None],
        norm_grads[0:1],
        norm_grads[1:2],
        norm_grads[2:3],
        norm_grads[3:4],
        qkv_total[None],
        out_total[None],
        up_total[None],
        down_total[None],
        skip_total[None],
    )


def solution(mesh):
    in_specs = (
        P(None, "dp", "tensor"),
        P(None, "dp", "tensor"),
        P(None, "dp", None),
        P("section", None),
        P("section", None),
        P("section", None),
        P("section", None),
        P("section", None, "tensor"),
        P("section", "tensor", None),
        P("section", None, "tensor"),
        P("section", "tensor", None),
        P("section", None, "tensor"),
    )
    out_specs = (
        P("section", None, "dp", "tensor"),
        P("section", None),
        P("section", None),
        P("section", None),
        P("section", None),
        P("section", None, "tensor"),
        P("section", "tensor", None),
        P("section", None, "tensor"),
        P("section", "tensor", None),
        P("section", None, "tensor"),
    )
    return jax.shard_map(shards, mesh=mesh, in_specs=in_specs, out_specs=out_specs, check_vma=False)
```

time: 907 us -> 513 us (0.57)
  waiting for transfers between devices: 523 us -> 215 us
  Pallas kernels: 0 us -> 134 us
  blocking collectives: 135 us -> 18.7 us
  matrix products: 97.5 us -> 2.84 us
  other arithmetic: 55.1 us -> 32.3 us
  local copies, waits for them, and re-layouts: 30.7 us -> 41.1 us
    reduce_scatter x15 -> x0, waiting for transfers between devices: 266 us -> none  [reduce_rows(): lax.psum_scatter(partial_sum.astype(jnp.bfloat16), 'tensor', scatter_dime...]
    psum x1, waiting for transfers between devices: 206 us -> 0.02 us  [over_dp(): return lax.psum(total.astype(jnp.bfloat16), 'dp').astype(jnp.float32)]
    pallas_call x0 -> x26, Pallas kernels: none -> 134 us  [the longest x16 33.5 us: call(): pl.pallas_call(kernel, out_shape=list(outs), in_specs=[SCALARS] * len(sca...]
    dot_general x63 -> x2, matrix products: 97.5 us -> 2.84 us  [the longest x1 1.54 us: dot_nt(): lax.dot_general(left, right, (((1,), (1,)), ((), ())), preferred_element_...]
    ppermute x8 -> x64, waiting for transfers between devices: 16 us -> 109 us  [the longest x16 70.1 us: x_swap(): return lax.ppermute(value, 'tensor', [(at, at ^ 2) for at in range(count)])]
    all_gather x2 -> x6, waiting for transfers between devices: 18.3 us -> 105 us  [the longest x4 105 us: all_rows(): return lax.all_gather(mine, ('dp', 'tensor'), axis=0, tiled=True)]
    all_gather x14 -> x2, blocking collectives: 96.2 us -> 18.7 us  [shards(): lax.all_gather(frames[m], 'tensor', axis=1, tiled=True)]
    psum x2 -> x0, blocking collectives: 31.3 us -> none  [the longest x1 19.3 us: shards(): lax.psum(gain_one.astype(jnp.bfloat16), 'dp').astype(jnp.float32)]
  transfers between devices with their start and end apart: 33 -> 71, of which waited for: 23 -> 30; matrix products, arithmetic and copies ran while one was open for 8% -> 7% of each run, Pallas kernels for 0% -> 21%
where the time goes in v1:
time: 513 us; the launch traced here: 505 us
  waiting for transfers between devices  215 us (42%)
  Pallas kernels  134 us (26%)
  starting transfers between devices  44.4 us (9%)
  local copies, waits for them, and re-layouts  41.1 us (8%)
  other arithmetic  32.3 us (6%)
  blocking collectives  18.7 us (4%)
  between operations  16.2 us (3%)
    all_gather x4, waiting for transfers between devices, all_rows(): return lax.all_gather(mine, ('dp', 'tensor'), axis=0, tiled=True)  105 us
    ppermute x16, waiting for transfers between devices, x_swap(): return lax.ppermute(value, 'tensor', [(at, at ^ 2) for at in range(count)])  70.1 us
    unnamed x243, local copies, waits for them, and re-layouts  39.2 us
    pallas_call x16, Pallas kernels, call(): pl.pallas_call(kernel, out_shape=list(outs), in_specs=[SCALARS] * len(sca...  33.5 us
    pallas_call x1, Pallas kernels, ffn_weights(): pl.pallas_call(ffn_weights_kernel, grid=(rows // block,), in_specs=[piece...  33.3 us
    ppermute x8, waiting for transfers between devices, section_swap(): return lax.ppermute(value, 'section', [(0, 1), (1, 0)])  30.3 us
    pallas_call x1, Pallas kernels, attn_weights(): pl.pallas_call(attn_weights_kernel, grid=(rows // block,), in_specs=[SCAL...  29.6 us
    pallas_call x4, Pallas kernels, ffn_forward(): pl.pallas_call(ffn_fwd_kernel, grid=(units // wide,), in_specs=[part, par...  20.8 us
  transfers between devices with their start and end apart: 71, of which 30 were waited for; matrix products, arithmetic and copies ran while one was open for 7% of the time, Pallas kernels for 21%

profile of v1, /device:TPU:0, one launch (start us, length us, event | category | flops | bytes accessed | tf_op | source)
XLA Modules:
  0.0 504.6 jit_solution(3303333174414288006)
XLA Ops:
  10.4 8.6 %all-gather.1 = bf16[1,256,1024]{2,1,0:T(8,128)(2,1)S(1)} all-gather(bf16[1,256,256]{2,1,0:T(8,128)(2,1)S(1)} %get-tuple-element.193), channel_id=3, replica_groups=mesh['section'=2,'dp'=4,'tensor'=4] {'tensor'}, dimensions={2}, use_global_device_ids=true | all-gather | bytes 655360 | tf_op jit(solution)/shard_map/all_gather | solution.py:546
  19.0 10.1 %all-gather = bf16[1,256,1024]{2,1,0:T(8,128)(2,1)S(1)} all-gather(bf16[1,256,256]{2,1,0:T(8,128)(2,1)S(1)} %get-tuple-element.192), channel_id=2, replica_groups=mesh['section'=2,'dp'=4,'tensor'=4] {'tensor'}, dimensions={2}, use_global_device_ids=true | all-gather | bytes 655360 | tf_op jit(solution)/shard_map/all_gather | solution.py:546
  30.9 2.4 shard_map.207
  35.9 2.4 shard_map.195
  41.5 6.4 %collective-permute-done.28 = bf16[128,1024]{1,0:T(8,128)(2,1)S(1)} collective-permute-done((bf16[128,1024]{1,0:T(8,128)(2,1)S(1)}, bf16[128,1024]{1,0:T(8,128)(2,1)S(1)}, u32[]{:S(2)}, u32[]{:S(2)}) %collective-permute-start.28) | collective-permute-done | bytes 262176 | tf_op jit(solution)/shard_map/ppermute | solution.py:28
  48.0 4.9 collective-permute-done.1
  53.1 5.0 shard_map.208
  59.7 5.0 shard_map.196
  70.2 5.6 %collective-permute-done.31 = bf16[128,1024]{1,0:T(8,128)(2,1)S(1)} collective-permute-done((bf16[128,1024]{1,0:T(8,128)(2,1)S(1)}, bf16[128,1024]{1,0:T(8,128)(2,1)S(1)}, u32[]{:S(2)}, u32[]{:S(2)}) %collective-permute-start.31) | collective-permute-done | bytes 262176 | tf_op jit(solution)/shard_map/ppermute | solution.py:28
  80.7 3.3 collective-permute-done.4
  88.0 3.7 collective-permute-done.33.skip_part
  92.2 5.1 %collective-permute-done.5.rows = bf16[128,1024]{1,0:T(8,128)(2,1)S(1)} collective-permute-done((bf16[128,1024]{1,0:T(8,128)(2,1)S(1)}, bf16[128,1024]{1,0:T(8,128)(2,1)S(1)}, u32[]{:S(2)}, u32[]{:S(2)}) %collective-permute-start.5) | collective-permute-done | bytes 262176 | tf_op jit(solution)/shard_map/ppermute | solution.py:32
  97.3 3.8 collective-permute-done.6.skip_part
  101.7 2.4 shard_map.211
  108.1 3.1 shard_map.199
  118.4 4.6 collective-permute-done.36
  124.2 3.9 collective-permute-done.9
  128.3 5.0 shard_map.212
  134.8 3.7 shard_map.213
  139.2 5.7 %shard_map.200 = (bf16[128,1024]{1,0:T(8,128)(2,1)S(1)}, f32[128,1024]{1,0:T(8,128)S(1)}, f32[256,1024]{1,0:T(8,128)S(1)}, bf16[128,1024]{1,0:T(8,128)(2,1)}, bf16[128,1024]{1,0:T(8,128)(2,1)S(1)}) custom-call(bf16[128,1024]{1,0:T(8,128)(2,1)S(1)} %copy-done.21, bf16[128,1024]{1,0:T(8,128)(2,1)S(1)} %copy-done.45, ...), custom_call_target="tpu_custom_call" | custom-call | flops 1073741824 | bytes 5242880 | tf_op jit(solution)/shard_map/pallas_call | solution.py:401
  146.4 3.8 shard_map.201
  153.4 6.2 %collective-permute-done.39 = bf16[128,1024]{1,0:T(8,128)(2,1)S(1)} collective-permute-done((bf16[128,1024]{1,0:T(8,128)(2,1)S(1)}, bf16[128,1024]{1,0:T(8,128)(2,1)S(1)}, u32[]{:S(2)}, u32[]{:S(2)}) %collective-permute-start.39) | collective-permute-done | bytes 262176 | tf_op jit(solution)/shard_map/ppermute | solution.py:28
  159.8 5.1 %collective-permute-done.12 = bf16[128,1024]{1,0:T(8,128)(2,1)S(1)} collective-permute-done((bf16[128,1024]{1,0:T(8,128)(2,1)S(1)}, bf16[128,1024]{1,0:T(8,128)(2,1)S(1)}, u32[]{:S(2)}, u32[]{:S(2)}) %collective-permute-start.12) | collective-permute-done | bytes 262176 | tf_op jit(solution)/shard_map/ppermute | solution.py:28
  165.6 3.6 shard_map.214
  181.1 4.0 shard_map.202
  189.4 6.7 %collective-permute-done.42.far = bf16[128,1024]{1,0:T(8,128)(2,1)S(1)} collective-permute-done((bf16[128,1024]{1,0:T(8,128)(2,1)S(1)}, bf16[128,1024]{1,0:T(8,128)(2,1)S(1)}, u32[]{:S(2)}, u32[]{:S(2)}) %collective-permute-start.42) | collective-permute-done | bytes 262176 | tf_op jit(solution)/shard_map/ppermute | solution.py:28
  199.0 2.2 collective-permute-done.15.far
  205.6 4.8 collective-permute-done.23.joined_grad
  217.9 7.4 %collective-permute-done.43.g_mine = bf16[128,1024]{1,0:T(8,128)(2,1)} collective-permute-done((bf16[128,1024]{1,0:T(8,128)(2,1)}, bf16[128,1024]{1,0:T(8,128)(2,1)}, u32[]{:S(2)}, u32[]{:S(2)}) %collective-permute-start.43) | collective-permute-done | bytes 262176 | tf_op jit(solution)/shard_map/ppermute | solution.py:32
  225.3 4.8 collective-permute-done.16.g_mine
  240.2 4.8 shard_map.216
  245.2 4.6 shard_map.204
  252.9 6.6 %collective-permute-done.46 = bf16[128,1024]{1,0:T(8,128)(2,1)S(1)} collective-permute-done((bf16[128,1024]{1,0:T(8,128)(2,1)S(1)}, bf16[128,1024]{1,0:T(8,128)(2,1)S(1)}, u32[]{:S(2)}, u32[]{:S(2)}) %collective-permute-start.46) | collective-permute-done | bytes 262176 | tf_op jit(solution)/shard_map/ppermute | solution.py:28
  259.7 4.7 collective-permute-done.19
  264.6 3.9 shard_map.217
  270.1 3.9 shard_map.205
  278.3 3.6 collective-permute-start.59
  297.7 2.1 broadcast_in_dim.51
  299.8 7.2 %collective-permute-done.49.far = bf16[128,1024]{1,0:T(8,128)(2,1)} collective-permute-done((bf16[128,1024]{1,0:T(8,128)(2,1)S(1)}, bf16[128,1024]{1,0:T(8,128)(2,1)}, u32[]{:S(2)}, u32[]{:S(2)}) %collective-permute-start.49) | collective-permute-done | bytes 262176 | tf_op jit(solution)/shard_map/ppermute | solution.py:28
  310.0 2.7 collective-permute-done.22.far
  312.7 1.9 shard_map.206
  320.4 2.4 collective-permute-start.56
  322.9 2.6 collective-permute-done.56
  326.9 36.0 %all-gather.19.cloned.1.call-done.grad_out = bf16[2048,1024]{1,0:T(8,128)(2,1)} async-done(((bf16[128,1024]{1,0:T(8,128)(2,1)}), bf16[2048,1024]{1,0:T(8,128)(2,1)}) %all-gather.19.cloned.1.call-update) | async-done | bytes 4194320 | tf_op jit(solution)/shard_map/all_gather | solution.py:648
  362.9 33.3 %shard_map.220 = (f32[1024,1024]{1,0:T(8,128)}, f32[1024,1024]{1,0:T(8,128)}) custom-call(bf16[2048,1024]{1,0:T(8,128)(2,1)} %all-gather.17.cloned.1.call-done.ffn_in, bf16[2048,1024]{1,0:T(8,128)(2,1)} %all-gather.19.cloned.1.call-done.grad_out, bf16[1024,1024]{1,0:T(8,128)(2,1)} %bitcast.46, bf16[1024,1024]{1,0:T(8,128)(2,1)} %bitcast.55), custom_call_target="tpu_custom_call" | custom-call | flops 17179869184 | bytes 16777216 | tf_op jit(solution)/shard_map/pallas_call | solution.py:471
  396.2 18.0 %all-gather.13.cloned.1.call-done.attn_in = bf16[2048,1024]{1,0:T(8,128)(2,1)} async-done(((bf16[128,1024]{1,0:T(8,128)(2,1)}), bf16[2048,1024]{1,0:T(8,128)(2,1)}) %all-gather.13.cloned.1.call-update) | async-done | bytes 4194320 | tf_op jit(solution)/shard_map/all_gather | solution.py:648
  414.2 51.2 %all-gather.15.cloned.1.call-done.grad_attn = bf16[2048,1024]{1,0:T(8,128)(2,1)} async-done(((bf16[128,1024]{1,0:T(8,128)(2,1)}), bf16[2048,1024]{1,0:T(8,128)(2,1)}) %all-gather.15.cloned.1.call-update) | async-done | bytes 4194320 | tf_op jit(solution)/shard_map/all_gather | solution.py:648
  467.8 29.6 %shard_map.219 = (f32[1024,768]{1,0:T(8,128)}, f32[256,1024]{1,0:T(8,128)}) custom-call(s32[3]{0:T(128)S(1)} %pad_add_fusion.2.here, s32[16]{0:T(128)S(1)} %pad_add_fusion.3.lens, f32[4]{0:T(128)S(1)} %multiply_power_fusion.slopes, bf16[2048,1024]{1,0:T(8,128)(2,1)} %all-gather.13.cloned.1.call-done.attn_in, ...), custom_call_target="tpu_custom_call" | custom-call | flops 15032385536 | bytes 6291456 | tf_op jit(solution)/shard_map/pallas_call | solution.py:488
  (443 shorter events, 126.0 us)
Async XLA Ops:
  7.2 70.9 %all-gather.11.cloned.1.call-start = ((), (), s32[]{:S(2)}) async-start(), calls=%async_computation.1 | async-start | bytes 2621440 | tf_op jit(solution)/shard_map/all_gather | solution.py:547
  7.9 107.0 %all-gather.9.cloned.1.call-start = ((), (), s32[]{:S(2)}) async-start(), calls=%async_computation | async-start | bytes 1310720 | tf_op jit(solution)/shard_map/all_gather | solution.py:548
  38.7 9.2 %collective-permute-start.28 = (bf16[128,1024]{1,0:T(8,128)(2,1)S(1)}, bf16[128,1024]{1,0:T(8,128)(2,1)S(1)}, u32[]{:S(2)}, u32[]{:S(2)}) collective-permute-start(bf16[128,1024]{1,0:T(8,128)(2,1)S(1)} %add_convert_fusion.13), channel_id=1, source_target_pairs={{0,2},{1,3},{2,0},{3,1},{4,6},{5,7},{6,4},{7,5},{8,10},{9,11},{10,... | collective-permute-start | bytes 786440 | tf_op jit(solution)/shard_map/ppermute | solution.py:28
  40.2 12.7 %collective-permute-start.1 = (bf16[128,1024]{1,0:T(8,128)(2,1)S(1)}, bf16[128,1024]{1,0:T(8,128)(2,1)S(1)}, u32[]{:S(2)}, u32[]{:S(2)}) collective-permute-start(bf16[128,1024]{1,0:T(8,128)(2,1)S(1)} %add_convert_fusion.27), channel_id=1, source_target_pairs={{0,2},{1,3},{2,0},{3,1},{4,6},{5,7},{6,4},{7,5},{8,10},{9,11},{10,... | collective-permute-start | bytes 786440 | tf_op jit(solution)/shard_map/ppermute | solution.py:28
  53.0 6.7 %collective-permute-start.2 = (bf16[128,1024]{1,0:T(8,128)(2,1)S(1)}, bf16[128,1024]{1,0:T(8,128)(2,1)S(1)}, u32[]{:S(2)}, u32[]{:S(2)}) collective-permute-start(bf16[128,1024]{1,0:T(8,128)(2,1)S(1)} %add_convert_fusion.26.s_mine), channel_id=1, source_target_pairs={{0,1},{1,0},{2,3},{3,2},{4,5},{5,4},{6,7},{7,6},{8,9},{9,8},{10,11... | collective-permute-start | bytes 786440 | tf_op jit(solution)/shard_map/ppermute | solution.py:23
  59.2 7.3 %collective-permute-start.30 = (bf16[128,1024]{1,0:T(8,128)(2,1)S(1)}, bf16[128,1024]{1,0:T(8,128)(2,1)S(1)}, u32[]{:S(2)}, u32[]{:S(2)}) collective-permute-start(bf16[128,1024]{1,0:T(8,128)(2,1)S(1)} %get-tuple-element.125), channel_id=1, source_target_pairs={{0,1},{1,0},{2,3},{3,2},{4,5},{5,4},{6,7},{7,6},{8,9},{9,8},{10,11... | collective-permute-start | bytes 786440 | tf_op jit(solution)/shard_map/ppermute | solution.py:23
  66.6 9.2 %collective-permute-start.31 = (bf16[128,1024]{1,0:T(8,128)(2,1)S(1)}, bf16[128,1024]{1,0:T(8,128)(2,1)S(1)}, u32[]{:S(2)}, u32[]{:S(2)}) collective-permute-start(bf16[128,1024]{1,0:T(8,128)(2,1)S(1)} %add_convert_fusion.11), channel_id=1, source_target_pairs={{0,2},{1,3},{2,0},{3,1},{4,6},{5,7},{6,4},{7,5},{8,10},{9,11},{10,... | collective-permute-start | bytes 786440 | tf_op jit(solution)/shard_map/ppermute | solution.py:28
  68.1 229.6 %all-reduce.2.cloned.1.call-start = ((), (), s32[]{:S(2)}) async-start(), calls=%async_computation.6 | async-start | bytes 1048576 | tf_op jit(solution)/shard_map/psum | solution.py:661
  69.4 14.7 %collective-permute-start.4 = (bf16[128,1024]{1,0:T(8,128)(2,1)}, bf16[128,1024]{1,0:T(8,128)(2,1)}, u32[]{:S(2)}, u32[]{:S(2)}) collective-permute-start(bf16[128,1024]{1,0:T(8,128)(2,1)} %add_convert_fusion.25), channel_id=1, source_target_pairs={{0,2},{1,3},{2,0},{3,1},{4,6},{5,7},{6,4},{7,5},{8,10},{9,11},{10,... | collective-permute-start | bytes 786440 | tf_op jit(solution)/shard_map/ppermute | solution.py:28
  76.6 11.4 %collective-permute-start.32 = (bf16[128,1024]{1,0:T(8,128)(2,1)}, bf16[128,1024]{1,0:T(8,128)(2,1)S(1)}, u32[]{:S(2)}, u32[]{:S(2)}) collective-permute-start(bf16[128,1024]{1,0:T(8,128)(2,1)} %add_convert_fusion.10), channel_id=1, source_target_pairs={{0,16},{16,0},{1,17},{17,1},{2,18},{18,2},{3,19},{19,3},{4,20},{20... | collective-permute-start | bytes 786440 | tf_op jit(solution)/shard_map/ppermute | solution.py:32
  80.1 11.5 %collective-permute-start.33 = (bf16[128,1024]{1,0:T(8,128)(2,1)S(1)}, bf16[128,1024]{1,0:T(8,128)(2,1)S(1)}, u32[]{:S(2)}, u32[]{:S(2)}) collective-permute-start(bf16[128,1024]{1,0:T(8,128)(2,1)S(1)} %shard_map.209), channel_id=1, source_target_pairs={{0,16},{16,0},{1,17},{17,1},{2,18},{18,2},{3,19},{19,3},{4,20},{20... | collective-permute-start | bytes 786440 | tf_op jit(solution)/shard_map/ppermute | solution.py:32
  85.4 11.9 %collective-permute-start.5 = (bf16[128,1024]{1,0:T(8,128)(2,1)S(1)}, bf16[128,1024]{1,0:T(8,128)(2,1)S(1)}, u32[]{:S(2)}, u32[]{:S(2)}) collective-permute-start(bf16[128,1024]{1,0:T(8,128)(2,1)S(1)} %add_convert_fusion.24), channel_id=1, source_target_pairs={{0,16},{16,0},{1,17},{17,1},{2,18},{18,2},{3,19},{19,3},{4,20},{20... | collective-permute-start | bytes 786440 | tf_op jit(solution)/shard_map/ppermute | solution.py:32
  87.4 13.7 %collective-permute-start.6 = (bf16[128,1024]{1,0:T(8,128)(2,1)S(1)}, bf16[128,1024]{1,0:T(8,128)(2,1)S(1)}, u32[]{:S(2)}, u32[]{:S(2)}) collective-permute-start(bf16[128,1024]{1,0:T(8,128)(2,1)S(1)} %shard_map.197), channel_id=1, source_target_pairs={{0,16},{16,0},{1,17},{17,1},{2,18},{18,2},{3,19},{19,3},{4,20},{20... | collective-permute-start | bytes 786440 | tf_op jit(solution)/shard_map/ppermute | solution.py:32
  92.1 9.5 %collective-permute-start.34 = (bf16[128,1024]{1,0:T(8,128)(2,1)S(1)}, bf16[128,1024]{1,0:T(8,128)(2,1)S(1)}, u32[]{:S(2)}, u32[]{:S(2)}) collective-permute-start(bf16[128,1024]{1,0:T(8,128)(2,1)S(1)} %shard_map.210.v_mine), channel_id=1, source_target_pairs={{0,1},{1,0},{2,3},{3,2},{4,5},{5,4},{6,7},{7,6},{8,9},{9,8},{10,11... | collective-permute-start | bytes 786440 | tf_op jit(solution)/shard_map/ppermute | solution.py:23
  101.6 6.5 %collective-permute-start.7 = (bf16[128,1024]{1,0:T(8,128)(2,1)S(1)}, bf16[128,1024]{1,0:T(8,128)(2,1)S(1)}, u32[]{:S(2)}, u32[]{:S(2)}) collective-permute-start(bf16[128,1024]{1,0:T(8,128)(2,1)S(1)} %shard_map.198.v_mine), channel_id=1, source_target_pairs={{0,1},{1,0},{2,3},{3,2},{4,5},{5,4},{6,7},{7,6},{8,9},{9,8},{10,11... | collective-permute-start | bytes 786440 | tf_op jit(solution)/shard_map/ppermute | solution.py:23
  106.3 6.5 %collective-permute-start.35 = (bf16[128,1024]{1,0:T(8,128)(2,1)S(1)}, bf16[128,1024]{1,0:T(8,128)(2,1)S(1)}, u32[]{:S(2)}, u32[]{:S(2)}) collective-permute-start(bf16[128,1024]{1,0:T(8,128)(2,1)S(1)} %get-tuple-element.127), channel_id=1, source_target_pairs={{0,1},{1,0},{2,3},{3,2},{4,5},{5,4},{6,7},{7,6},{8,9},{9,8},{10,11... | collective-permute-start | bytes 786440 | tf_op jit(solution)/shard_map/ppermute | solution.py:23
  113.6 9.4 %collective-permute-start.36 = (bf16[128,1024]{1,0:T(8,128)(2,1)}, bf16[128,1024]{1,0:T(8,128)(2,1)}, u32[]{:S(2)}, u32[]{:S(2)}) collective-permute-start(bf16[128,1024]{1,0:T(8,128)(2,1)} %add_convert_fusion.9), channel_id=1, source_target_pairs={{0,2},{1,3},{2,0},{3,1},{4,6},{5,7},{6,4},{7,5},{8,10},{9,11},{10,... | collective-permute-start | bytes 786440 | tf_op jit(solution)/shard_map/ppermute | solution.py:28
  117.7 10.4 %collective-permute-start.9 = (bf16[128,1024]{1,0:T(8,128)(2,1)S(1)}, bf16[128,1024]{1,0:T(8,128)(2,1)S(1)}, u32[]{:S(2)}, u32[]{:S(2)}) collective-permute-start(bf16[128,1024]{1,0:T(8,128)(2,1)S(1)} %add_convert_fusion.23), channel_id=1, source_target_pairs={{0,2},{1,3},{2,0},{3,1},{4,6},{5,7},{6,4},{7,5},{8,10},{9,11},{10,... | collective-permute-start | bytes 786440 | tf_op jit(solution)/shard_map/ppermute | solution.py:28
  128.2 10.9 %collective-permute-start.10 = (bf16[128,1024]{1,0:T(8,128)(2,1)S(1)}, bf16[128,1024]{1,0:T(8,128)(2,1)S(1)}, u32[]{:S(2)}, u32[]{:S(2)}) collective-permute-start(bf16[128,1024]{1,0:T(8,128)(2,1)S(1)} %add_convert_fusion.22.s_mine), channel_id=1, source_target_pairs={{0,1},{1,0},{2,3},{3,2},{4,5},{5,4},{6,7},{7,6},{8,9},{9,8},{10,11... | collective-permute-start | bytes 786440 | tf_op jit(solution)/shard_map/ppermute | solution.py:23
  138.5 11.9 %collective-permute-start.38 = (bf16[128,1024]{1,0:T(8,128)(2,1)S(1)}, bf16[128,1024]{1,0:T(8,128)(2,1)S(1)}, u32[]{:S(2)}, u32[]{:S(2)}) collective-permute-start(bf16[128,1024]{1,0:T(8,128)(2,1)S(1)} %get-tuple-element.130), channel_id=1, source_target_pairs={{0,1},{1,0},{2,3},{3,2},{4,5},{5,4},{6,7},{7,6},{8,9},{9,8},{10,11... | collective-permute-start | bytes 786440 | tf_op jit(solution)/shard_map/ppermute | solution.py:23
  150.5 9.2 %collective-permute-start.39 = (bf16[128,1024]{1,0:T(8,128)(2,1)S(1)}, bf16[128,1024]{1,0:T(8,128)(2,1)S(1)}, u32[]{:S(2)}, u32[]{:S(2)}) collective-permute-start(bf16[128,1024]{1,0:T(8,128)(2,1)S(1)} %add_convert_fusion.7), channel_id=1, source_target_pairs={{0,2},{1,3},{2,0},{3,1},{4,6},{5,7},{6,4},{7,5},{8,10},{9,11},{10,... | collective-permute-start | bytes 786440 | tf_op jit(solution)/shard_map/ppermute | solution.py:28
  152.0 12.9 %collective-permute-start.12 = (bf16[128,1024]{1,0:T(8,128)(2,1)S(1)}, bf16[128,1024]{1,0:T(8,128)(2,1)S(1)}, u32[]{:S(2)}, u32[]{:S(2)}) collective-permute-start(bf16[128,1024]{1,0:T(8,128)(2,1)S(1)} %add_convert_fusion.21), channel_id=1, source_target_pairs={{0,2},{1,3},{2,0},{3,1},{4,6},{5,7},{6,4},{7,5},{8,10},{9,11},{10,... | collective-permute-start | bytes 786440 | tf_op jit(solution)/shard_map/ppermute | solution.py:28
  159.7 5.9 %collective-permute-start.40 = (bf16[128,1024]{1,0:T(8,128)(2,1)S(1)}, bf16[128,1024]{1,0:T(8,128)(2,1)S(1)}, u32[]{:S(2)}, u32[]{:S(2)}) collective-permute-start(bf16[128,1024]{1,0:T(8,128)(2,1)S(1)} %add_convert_fusion.6.t_mine), channel_id=1, source_target_pairs={{0,1},{1,0},{2,3},{3,2},{4,5},{5,4},{6,7},{7,6},{8,9},{9,8},{10,11... | collective-permute-start | bytes 786440 | tf_op jit(solution)/shard_map/ppermute | solution.py:23
  165.6 6.3 %collective-permute-start.13 = (bf16[128,1024]{1,0:T(8,128)(2,1)}, bf16[128,1024]{1,0:T(8,128)(2,1)}, u32[]{:S(2)}, u32[]{:S(2)}) collective-permute-start(bf16[128,1024]{1,0:T(8,128)(2,1)} %add_convert_fusion.20.t_mine), channel_id=1, source_target_pairs={{0,1},{1,0},{2,3},{3,2},{4,5},{5,4},{6,7},{7,6},{8,9},{9,8},{10,11... | collective-permute-start | bytes 786440 | tf_op jit(solution)/shard_map/ppermute | solution.py:23
  171.5 14.4 %collective-permute-start.41 = (bf16[128,1024]{1,0:T(8,128)(2,1)}, bf16[128,1024]{1,0:T(8,128)(2,1)}, u32[]{:S(2)}, u32[]{:S(2)}) collective-permute-start(bf16[128,1024]{1,0:T(8,128)(2,1)} %get-tuple-element.134), channel_id=1, source_target_pairs={{0,1},{1,0},{2,3},{3,2},{4,5},{5,4},{6,7},{7,6},{8,9},{9,8},{10,11... | collective-permute-start | bytes 786440 | tf_op jit(solution)/shard_map/ppermute | solution.py:23
  186.9 9.2 %collective-permute-start.42 = (bf16[128,1024]{1,0:T(8,128)(2,1)S(1)}, bf16[128,1024]{1,0:T(8,128)(2,1)S(1)}, u32[]{:S(2)}, u32[]{:S(2)}) collective-permute-start(bf16[128,1024]{1,0:T(8,128)(2,1)S(1)} %add_convert_fusion.5.near), channel_id=1, source_target_pairs={{0,2},{1,3},{2,0},{3,1},{4,6},{5,7},{6,4},{7,5},{8,10},{9,11},{10,... | collective-permute-start | bytes 786440 | tf_op jit(solution)/shard_map/ppermute | solution.py:28
  188.4 22.9 %collective-permute-start.61 = (bf16[128,1024]{1,0:T(8,128)(2,1)S(1)}, bf16[128,1024]{1,0:T(8,128)(2,1)S(1)}, u32[]{:S(2)}, u32[]{:S(2)}) collective-permute-start(bf16[128,1024]{1,0:T(8,128)(2,1)S(1)} %broadcast_select_fusion.2), channel_id=1, source_target_pairs={{0,1},{1,0},{2,3},{3,2},{4,5},{5,4},{6,7},{7,6},{8,9},{9,8},{10,11... | collective-permute-start | bytes 786440 | tf_op jit(solution)/shard_map/ppermute | solution.py:23
  188.7 12.6 %collective-permute-start.15 = (bf16[128,1024]{1,0:T(8,128)(2,1)S(1)}, bf16[128,1024]{1,0:T(8,128)(2,1)S(1)}, u32[]{:S(2)}, u32[]{:S(2)}) collective-permute-start(bf16[128,1024]{1,0:T(8,128)(2,1)S(1)} %add_convert_fusion.19.near), channel_id=1, source_target_pairs={{0,2},{1,3},{2,0},{3,1},{4,6},{5,7},{6,4},{7,5},{8,10},{9,11},{10,... | collective-permute-start | bytes 786440 | tf_op jit(solution)/shard_map/ppermute | solution.py:28
  197.3 7.5 %collective-permute-start.50 = (bf16[128,1024]{1,0:T(8,128)(2,1)S(1)}, bf16[128,1024]{1,0:T(8,128)(2,1)S(1)}, u32[]{:S(2)}, u32[]{:S(2)}) collective-permute-start(bf16[128,1024]{1,0:T(8,128)(2,1)S(1)} %get-tuple-element.145), channel_id=1, source_target_pairs={{0,16},{16,0},{1,17},{17,1},{2,18},{18,2},{3,19},{19,3},{4,20},{20... | collective-permute-start | bytes 786440 | tf_op jit(solution)/shard_map/ppermute | solution.py:32
  198.9 12.4 %collective-permute-start.60 = (bf16[128,1024]{1,0:T(8,128)(2,1)S(1)}, bf16[128,1024]{1,0:T(8,128)(2,1)S(1)}, u32[]{:S(2)}, u32[]{:S(2)}) collective-permute-start(bf16[128,1024]{1,0:T(8,128)(2,1)S(1)} %broadcast_select_fusion.3), channel_id=1, source_target_pairs={{0,1},{1,0},{2,3},{3,2},{4,5},{5,4},{6,7},{7,6},{8,9},{9,8},{10,11... | collective-permute-start | bytes 786440 | tf_op jit(solution)/shard_map/ppermute | solution.py:23
  202.5 7.9 %collective-permute-start.23 = (bf16[128,1024]{1,0:T(8,128)(2,1)S(1)}, bf16[128,1024]{1,0:T(8,128)(2,1)S(1)}, u32[]{:S(2)}, u32[]{:S(2)}) collective-permute-start(bf16[128,1024]{1,0:T(8,128)(2,1)S(1)} %get-tuple-element.116), channel_id=1, source_target_pairs={{0,16},{16,0},{1,17},{17,1},{2,18},{18,2},{3,19},{19,3},{4,20},{20... | collective-permute-start | bytes 786440 | tf_op jit(solution)/shard_map/ppermute | solution.py:32
  213.9 113.0 %all-gather.17.cloned.1.call-start = ((), (), s32[]{:S(2)}) async-start(), calls=%async_computation.4 | async-start | bytes 4456448 | tf_op jit(solution)/shard_map/all_gather | solution.py:648
  215.8 147.2 %all-gather.19.cloned.1.call-start = ((), (), s32[]{:S(2)}) async-start(), calls=%async_computation.5 | async-start | bytes 4456448 | tf_op jit(solution)/shard_map/all_gather | solution.py:648
  215.8 9.5 %collective-permute-start.43 = (bf16[128,1024]{1,0:T(8,128)(2,1)}, bf16[128,1024]{1,0:T(8,128)(2,1)}, u32[]{:S(2)}, u32[]{:S(2)}) collective-permute-start(bf16[128,1024]{1,0:T(8,128)(2,1)} %copy-done.116), channel_id=1, source_target_pairs={{0,16},{16,0},{1,17},{17,1},{2,18},{18,2},{3,19},{19,3},{4,20},{20... | collective-permute-start | bytes 786440 | tf_op jit(solution)/shard_map/ppermute | solution.py:32
  217.4 12.8 %collective-permute-start.16 = (bf16[128,1024]{1,0:T(8,128)(2,1)}, bf16[128,1024]{1,0:T(8,128)(2,1)}, u32[]{:S(2)}, u32[]{:S(2)}) collective-permute-start(bf16[128,1024]{1,0:T(8,128)(2,1)} %copy-done.118), channel_id=1, source_target_pairs={{0,16},{16,0},{1,17},{17,1},{2,18},{18,2},{3,19},{19,3},{4,20},{20... | collective-permute-start | bytes 786440 | tf_op jit(solution)/shard_map/ppermute | solution.py:32
  232.0 182.2 %all-gather.13.cloned.1.call-start = ((), (), s32[]{:S(2)}) async-start(), calls=%async_computation.2 | async-start | bytes 4456448 | tf_op jit(solution)/shard_map/all_gather | solution.py:648
  233.9 231.5 %all-gather.15.cloned.1.call-start = ((), (), s32[]{:S(2)}) async-start(), calls=%async_computation.3 | async-start | bytes 4456448 | tf_op jit(solution)/shard_map/all_gather | solution.py:648
  234.0 11.1 %collective-permute-start.17 = (bf16[128,1024]{1,0:T(8,128)(2,1)}, bf16[128,1024]{1,0:T(8,128)(2,1)S(1)}, u32[]{:S(2)}, u32[]{:S(2)}) collective-permute-start(bf16[128,1024]{1,0:T(8,128)(2,1)} %collective-permute-done.16.g_mine), channel_id=1, source_target_pairs={{0,1},{1,0},{2,3},{3,2},{4,5},{5,4},{6,7},{7,6},{8,9},{9,8},{10,11... | collective-permute-start | bytes 786440 | tf_op jit(solution)/shard_map/ppermute | solution.py:23
  250.3 9.2 %collective-permute-start.46 = (bf16[128,1024]{1,0:T(8,128)(2,1)S(1)}, bf16[128,1024]{1,0:T(8,128)(2,1)S(1)}, u32[]{:S(2)}, u32[]{:S(2)}) collective-permute-start(bf16[128,1024]{1,0:T(8,128)(2,1)S(1)} %add_convert_fusion.4), channel_id=1, source_target_pairs={{0,2},{1,3},{2,0},{3,1},{4,6},{5,7},{6,4},{7,5},{8,10},{9,11},{10,... | collective-permute-start | bytes 786440 | tf_op jit(solution)/shard_map/ppermute | solution.py:28
  251.8 12.5 %collective-permute-start.19 = (bf16[128,1024]{1,0:T(8,128)(2,1)S(1)}, bf16[128,1024]{1,0:T(8,128)(2,1)S(1)}, u32[]{:S(2)}, u32[]{:S(2)}) collective-permute-start(bf16[128,1024]{1,0:T(8,128)(2,1)S(1)} %add_convert_fusion.18), channel_id=1, source_target_pairs={{0,2},{1,3},{2,0},{3,1},{4,6},{5,7},{6,4},{7,5},{8,10},{9,11},{10,... | collective-permute-start | bytes 786440 | tf_op jit(solution)/shard_map/ppermute | solution.py:28
  278.3 6.5 %collective-permute-start.59 = (s32[4]{0:T(128)S(1)}, s32[4]{0:T(128)S(1)}, u32[]{:S(2)}, u32[]{:S(2)}) collective-permute-start(s32[4]{0:T(128)S(1)} %reshape.187), channel_id=1, source_target_pairs={{0,12},{4,0},{8,4},{12,8},{1,13},{5,1},{9,5},{13,9},{2,14},{6,2},{... | collective-permute-start | bytes 56 | tf_op jit(solution)/shard_map/ppermute | solution.py:42
  284.3 6.6 %collective-permute-start.48 = (bf16[128,1024]{1,0:T(8,128)(2,1)S(1)}, bf16[128,1024]{1,0:T(8,128)(2,1)S(1)}, u32[]{:S(2)}, u32[]{:S(2)}) collective-permute-start(bf16[128,1024]{1,0:T(8,128)(2,1)S(1)} %copy-done.115), channel_id=1, source_target_pairs={{0,1},{1,0},{2,3},{3,2},{4,5},{5,4},{6,7},{7,6},{8,9},{9,8},{10,11... | collective-permute-start | bytes 786440 | tf_op jit(solution)/shard_map/ppermute | solution.py:23
  287.4 7.8 %collective-permute-start.24 = (bf16[128,1024]{1,0:T(8,128)(2,1)}, bf16[128,1024]{1,0:T(8,128)(2,1)S(1)}, u32[]{:S(2)}, u32[]{:S(2)}) collective-permute-start(bf16[128,1024]{1,0:T(8,128)(2,1)} %get-tuple-element.120), channel_id=1, source_target_pairs={{0,1},{1,0},{2,3},{3,2},{4,5},{5,4},{6,7},{7,6},{8,9},{9,8},{10,11... | collective-permute-start | bytes 786440 | tf_op jit(solution)/shard_map/ppermute | solution.py:23
  289.6 25.1 %collective-permute-start.52 = (bf16[128,1024]{1,0:T(8,128)(2,1)}, bf16[128,1024]{1,0:T(8,128)(2,1)}, u32[]{:S(2)}, u32[]{:S(2)}) collective-permute-start(bf16[128,1024]{1,0:T(8,128)(2,1)} %add_convert_fusion.1), channel_id=1, source_target_pairs={{0,2},{1,3},{2,0},{3,1},{4,6},{5,7},{6,4},{7,5},{8,10},{9,11},{10,... | collective-permute-start | bytes 786440 | tf_op jit(solution)/shard_map/ppermute | solution.py:28
  292.0 15.1 %collective-permute-start.49 = (bf16[128,1024]{1,0:T(8,128)(2,1)S(1)}, bf16[128,1024]{1,0:T(8,128)(2,1)}, u32[]{:S(2)}, u32[]{:S(2)}) collective-permute-start(bf16[128,1024]{1,0:T(8,128)(2,1)S(1)} %add_convert_fusion.2.near), channel_id=1, source_target_pairs={{0,2},{1,3},{2,0},{3,1},{4,6},{5,7},{6,4},{7,5},{8,10},{9,11},{10,... | collective-permute-start | bytes 786440 | tf_op jit(solution)/shard_map/ppermute | solution.py:28
  293.8 18.9 %collective-permute-start.22 = (bf16[128,1024]{1,0:T(8,128)(2,1)S(1)}, bf16[128,1024]{1,0:T(8,128)(2,1)}, u32[]{:S(2)}, u32[]{:S(2)}) collective-permute-start(bf16[128,1024]{1,0:T(8,128)(2,1)S(1)} %add_convert_fusion.16.near), channel_id=1, source_target_pairs={{0,2},{1,3},{2,0},{3,1},{4,6},{5,7},{6,4},{7,5},{8,10},{9,11},{10,... | collective-permute-start | bytes 786440 | tf_op jit(solution)/shard_map/ppermute | solution.py:28
  296.9 21.2 %collective-permute-start.25 = (bf16[128,1024]{1,0:T(8,128)(2,1)}, bf16[128,1024]{1,0:T(8,128)(2,1)}, u32[]{:S(2)}, u32[]{:S(2)}) collective-permute-start(bf16[128,1024]{1,0:T(8,128)(2,1)} %add_convert_fusion.15), channel_id=1, source_target_pairs={{0,2},{1,3},{2,0},{3,1},{4,6},{5,7},{6,4},{7,5},{8,10},{9,11},{10,... | collective-permute-start | bytes 786440 | tf_op jit(solution)/shard_map/ppermute | solution.py:28
  316.0 10.1 %collective-permute-start.53 = (bf16[128,256]{1,0:T(8,128)(2,1)S(1)}, bf16[128,256]{1,0:T(8,128)(2,1)S(1)}, u32[]{:S(2)}, u32[]{:S(2)}) collective-permute-start(bf16[128,256]{1,0:T(8,128)(2,1)S(1)} %get-tuple-element.195), channel_id=1, source_target_pairs={{0,1},{1,0},{2,3},{3,2},{4,5},{5,4},{6,7},{7,6},{8,9},{9,8},{10,11... | collective-permute-start | bytes 196616 | tf_op jit(solution)/shard_map/ppermute | solution.py:23
  (144 other events, 1053.8 us)
Sparse Core Ops, SparseCore 0:
  9.6 28.0 all-gather.10
  68.2 19.9 all-gather.8
  214.0 39.4 all-reduce.1
  255.5 53.8 all-gather.16
  311.3 51.5 all-gather.18
  364.9 49.2 all-gather.12
  416.3 49.0 all-gather.14
